TPU v7x, 512 devices: a whole 4x4x16 slice. The times are simulated.
512 devices in a mesh: seq: 64 (over z_hi, x, y), chan: 4 (over z_lo), dp: 2 (over core).
Axes of the slice: x: 4, y: 4, z: 16 (z_hi: 4, z_lo: 4; z = z_hi * 4 + z_lo), core: 2. Of those that a mesh axis runs over, the one named last changes fastest.
Arguments:
- projected: float32 [3, 4, 4096, 4096], P(None, 'dp', 'seq', 'chan'), may hold values from -6 to 6
- short_weight: float32 [3, 7, 4096], P(None, None, 'chan'), may hold values from -2 to 2
- decay_rates: float32 [4096], P('chan'), may hold values from 1.2207031e-05 to 0.03125
- first_weight: float32 [32, 64], replicated, may hold values from -1 to 1
- second_weight: float32 [64, 64], replicated, may hold values from -0.75 to 0.75
- out_weight: float32 [64, 4096], P(None, 'chan'), may hold values from -0.75 to 0.75
- cotangent: float32 [4, 4096, 4096], P('dp', 'seq', 'chan'), may hold values from -6 to 6
Outputs:
- mixed: float32 [4, 4096, 4096], P('dp', 'seq', 'chan')
- raw_grad: float32 [3, 4, 4096, 4096], P(None, 'dp', 'seq', 'chan')
- short_grad: float32 [3, 7, 4096], P(None, None, 'chan')
- out_grad: float32 [64, 4096], P(None, 'chan')
- first_grad: float32 [32, 64], replicated
- second_grad: float32 [64, 64], replicated
All inputs are finite; a program needn't handle non-finite values.
Results may differ from a plain program's by a relative error of at most 0.00011.
Values sent between devices are 32-bit elements; how exact they have to be, the bound alone decides.
A program may use at most 64 MiB of HBM per device.

v0:
```python
import math

import jax
import jax.numpy as jnp
from jax import lax
from jax.sharding import PartitionSpec as P

precise = lax.Precision.HIGHEST


def passed_along(value, axis, steps):
    count = lax.axis_size(axis)
    leading, last = (max(0, -steps), min(count, count - steps))
    return lax.ppermute(value, axis, [(source, source + steps) for source in range(leading, last)])


def positional(positions, seq_len, count):
    half = count // 2
    orders = jnp.arange(half, dtype=jnp.int32)
    spread = max((half - 1) ** 2, 1)
    factors = 1 + (seq_len // 2 - 2) * orders * orders // spread
    phase = positions[:, None] * factors[None, :] % seq_len
    angle = phase.astype(jnp.float32) * (2.0 * math.pi / seq_len)
    return jnp.concatenate([jnp.cos(angle), jnp.sin(angle)], axis=1)


def envelope_of(steps_float, rates, seq_len):
    return (
        jnp.exp(-rates[None, :] * steps_float[:, None])
        * jnp.sqrt(2.0 * rates + 1.0 / seq_len)[None, :]
    )


def dft_tables(seq_len):
    inner = min(128, seq_len)
    outer = 2 * seq_len // inner
    half = seq_len // inner
    total = 2 * seq_len
    outer_idx = jnp.arange(outer, dtype=jnp.int32)
    half_idx = jnp.arange(half, dtype=jnp.int32)
    inner_idx = jnp.arange(inner, dtype=jnp.int32)
    first = (outer_idx[:, None] * half_idx[None, :] % outer).astype(jnp.float32) * (
        2.0 * math.pi / outer
    )
    twist = (outer_idx[:, None] * inner_idx[None, :] % total).astype(jnp.float32) * (
        2.0 * math.pi / total
    )
    second = (inner_idx[:, None] * inner_idx[None, :] % inner).astype(jnp.float32) * (
        2.0 * math.pi / inner
    )
    cos_first, sin_first = (jnp.cos(first), jnp.sin(first))
    cos_second, sin_second = (jnp.cos(second), jnp.sin(second))
    first_stack = jnp.stack([cos_first, -sin_first])
    forward_second = jnp.stack(
        [jnp.stack([cos_second, -sin_second]), jnp.stack([sin_second, cos_second])]
    )
    inverse_second = jnp.stack(
        [jnp.stack([cos_second, sin_second]), jnp.stack([-sin_second, cos_second])]
    )
    return (first_stack, jnp.cos(twist), jnp.sin(twist), forward_second, inverse_second)


def spectrum(signal, tables):
    first_stack, cos_twist, sin_twist, forward_second, inverse_second = tables
    batch, seq_len, chans = signal.shape
    half = first_stack.shape[2]
    inner = cos_twist.shape[1]
    folded = signal.reshape(batch, half, inner, chans)
    part = jnp.einsum("rkn,bnmc->rbckm", first_stack, folded, precision=precise)
    turned = jnp.stack(
        [part[0] * cos_twist + part[1] * sin_twist, part[1] * cos_twist - part[0] * sin_twist]
    )
    return jnp.einsum("rbckm,rsmj->sbckj", turned, forward_second, precision=precise)


def restore(freq, tables):
    first_stack, cos_twist, sin_twist, forward_second, inverse_second = tables
    outer = cos_twist.shape[0]
    inner = cos_twist.shape[1]
    half = first_stack.shape[2]
    back = jnp.einsum("rbckj,rsjm->sbckm", freq, inverse_second, precision=precise)
    turned = jnp.stack(
        [back[0] * cos_twist - back[1] * sin_twist, back[1] * cos_twist + back[0] * sin_twist]
    )
    signal = jnp.einsum("rkn,rbckm->bnmc", first_stack, turned, precision=precise)
    batch = signal.shape[0]
    chans = signal.shape[3]
    return signal.reshape(batch, half * inner, chans) / (outer * inner)


def owner_forward(prod_own, kern_freq, tables):
    prod_freq = spectrum(prod_own, tables)
    conv = jnp.stack(
        [
            prod_freq[0] * kern_freq[0] - prod_freq[1] * kern_freq[1],
            prod_freq[0] * kern_freq[1] + prod_freq[1] * kern_freq[0],
        ]
    )
    return (restore(conv, tables), prod_freq)


def owner_backward(grad_own, prod_freq, kern_freq, tables):
    grad_freq = spectrum(grad_own, tables)
    back = jnp.stack(
        [
            kern_freq[0] * grad_freq[0] + kern_freq[1] * grad_freq[1],
            kern_freq[0] * grad_freq[1] - kern_freq[1] * grad_freq[0],
        ]
    )
    corr = jnp.stack(
        [
            jnp.sum(
                prod_freq[0] * grad_freq[0] + prod_freq[1] * grad_freq[1], axis=0, keepdims=True
            ),
            jnp.sum(
                prod_freq[0] * grad_freq[1] - prod_freq[1] * grad_freq[0], axis=0, keepdims=True
            ),
        ]
    )
    return (restore(back, tables), restore(corr, tables))


def taps_behind(extended, weight, rows, rim):
    total = weight[:, 0][:, None, None, :] * extended[:, :, rim : rim + rows]
    for offset in range(1, rim + 1):
        total = (
            total
            + weight[:, offset][:, None, None, :]
            * extended[:, :, rim - offset : rim - offset + rows]
        )
    return total


def taps_ahead(extended, weight, rows, rim):
    total = weight[:, 0][:, None, None, :] * extended[:, :, 0:rows]
    for offset in range(1, rim + 1):
        total = total + weight[:, offset][:, None, None, :] * extended[:, :, offset : offset + rows]
    return total


def shards(
    projected, short_weight, decay_rates, first_weight, second_weight, out_weight, cotangent
):
    windows = projected.shape[1]
    rows = projected.shape[2]
    group = projected.shape[3]
    seq_count = lax.axis_size("seq")
    seq_len = rows * seq_count
    width = group * lax.axis_size("chan")
    all_windows = windows * lax.axis_size("dp")
    rim = short_weight.shape[1] - 1
    place = lax.axis_index("seq")
    tables = dft_tables(seq_len)
    last_rows = projected[:, :, rows - rim :, :]
    earlier = passed_along(last_rows, "seq", 1)
    extended = jnp.concatenate([earlier, projected], axis=2)
    featured = taps_behind(extended, short_weight, rows, rim)
    feat_q, feat_k, feat_v = (featured[0], featured[1], featured[2])
    product = feat_k * feat_v
    grad_conv = cotangent * feat_q
    positions = place * rows + jnp.arange(rows, dtype=jnp.int32)
    embedded = positional(positions, seq_len, first_weight.shape[0])
    first_pre = jnp.dot(
        embedded, first_weight, precision=precise, preferred_element_type=jnp.float32
    )
    first_act = jnp.sin(first_pre)
    second_pre = jnp.dot(
        first_act, second_weight, precision=precise, preferred_element_type=jnp.float32
    )
    second_act = jnp.sin(second_pre)
    envelope = envelope_of(positions.astype(jnp.float32), decay_rates, seq_len)
    kernel = (
        jnp.dot(second_act, out_weight, precision=precise, preferred_element_type=jnp.float32)
        * envelope
    )[None]
    kernel_own = lax.all_to_all(kernel, "seq", split_axis=2, concat_axis=1, tiled=True)
    kern_freq = spectrum(kernel_own, tables)
    prod_own = lax.all_to_all(product, "seq", split_axis=2, concat_axis=1, tiled=True)
    conv_own, prod_freq = owner_forward(prod_own, kern_freq, tables)
    convolved = lax.all_to_all(conv_own, "seq", split_axis=1, concat_axis=2, tiled=True)
    grad_own = lax.all_to_all(grad_conv, "seq", split_axis=2, concat_axis=1, tiled=True)
    back_own, kern_grad_own = owner_backward(grad_own, prod_freq, kern_freq, tables)
    grad_prod = lax.all_to_all(back_own, "seq", split_axis=1, concat_axis=2, tiled=True)
    mixed = feat_q * convolved
    grad_feat = jnp.stack([cotangent * convolved, grad_prod * feat_v, grad_prod * feat_k])
    first_rows = grad_feat[:, :, :rim]
    later = passed_along(first_rows, "seq", -1)
    ahead = jnp.concatenate([grad_feat, later], axis=2)
    raw_grad = taps_ahead(ahead, short_weight, rows, rim)
    short_local = jnp.stack(
        [
            jnp.sum(grad_feat * extended[:, :, rim - offset : rim - offset + rows], axis=(1, 2))
            for offset in range(rim + 1)
        ],
        axis=1,
    )
    tail_scale = 1.0 / math.sqrt(all_windows * seq_len)
    kernel_back = lax.all_to_all(kern_grad_own, "seq", split_axis=1, concat_axis=2, tiled=True)
    kernel_grad = kernel_back[0] * envelope
    out_part = jnp.dot(
        second_act.T, kernel_grad, precision=precise, preferred_element_type=jnp.float32
    )
    act_grad = jnp.dot(
        kernel_grad, out_weight.T, precision=precise, preferred_element_type=jnp.float32
    )
    short_total, out_total = lax.psum((short_local, out_part), ("seq", "dp"))
    second_grad_pre = act_grad * jnp.cos(second_pre)
    second_part = jnp.dot(
        first_act.T, second_grad_pre, precision=precise, preferred_element_type=jnp.float32
    )
    first_grad_pre = jnp.dot(
        second_grad_pre, second_weight.T, precision=precise, preferred_element_type=jnp.float32
    ) * jnp.cos(first_pre)
    first_part = jnp.dot(
        embedded.T, first_grad_pre, precision=precise, preferred_element_type=jnp.float32
    )
    first_total, second_total = lax.psum((first_part, second_part), ("seq", "chan", "dp"))
    grad_scale = 4.0 / math.sqrt(all_windows * seq_len * width)
    return (
        mixed,
        raw_grad,
        short_total * tail_scale,
        out_total * tail_scale,
        first_total * grad_scale,
        second_total * grad_scale,
    )


def solution(mesh):
    return jax.shard_map(
        shards,
        mesh=mesh,
        in_specs=(
            P(None, "dp", "seq", "chan"),
            P(None, None, "chan"),
            P("chan"),
            P(),
            P(),
            P(None, "chan"),
            P("dp", "seq", "chan"),
        ),
        out_specs=(
            P("dp", "seq", "chan"),
            P(None, "dp", "seq", "chan"),
            P(None, None, "chan"),
            P(None, "chan"),
            P(),
            P(),
        ),
        check_vma=False,
    )
```

profile of v0, /device:TPU:1, one launch (start us, length us, event | category | flops | bytes accessed | tf_op | source)
XLA Modules:
  0.0 1881.6 jit_solution(9026330579546238398)
XLA Ops:
  8.3 4.0 collective-permute-start
  20.8 21.1 %all-to-all-start.1 = ((f32[64,1,1024]{2,1,0:T(1,128)}), f32[64,1,1024]{2,1,0:T(1,128)}, u32[]{:S(2)}, u32[]{:S(2)}) async-start(f32[64,1,1024]{2,1,0:T(1,128)} %reshape.341), calls=%async_computation.1 | async-start | bytes 524288 | tf_op jit(solution)/shard_map/all_to_all | solution.py:176
  46.3 12.9 all-to-all-done.1
  59.1 11.4 all-to-all-start.3
  73.1 19.6 %all-to-all-done.3 = f32[64,1,2048]{2,1,0:T(1,128)} async-done(((f32[64,1,2048]{2,1,0:T(1,128)}), f32[64,1,2048]{2,1,0:T(1,128)}, u32[]{:S(2)}, u32[]{:S(2)}) %all-to-all-start.3) | async-done | bytes 524320 | tf_op jit(solution)/shard_map/all_to_all | solution.py:181
  92.7 12.2 all-to-all-start
  112.3 3.7 reduce.2
  119.2 3.9 all-to-all-done
  123.1 3.7 reduce.3
  145.9 20.3 %reduce.8 = f32[4096,16]{1,0:T(8,128)} reduce(f32[4096,1,16]{2,1,0:T(1,128)} %bitcast.280, f32[]{:T(128)} %broadcast.390), dimensions={1}, to_apply=%bitcast.256.reduce_sub_computation | reduce | bytes 524292
  169.2 13.5 all-to-all-start.5
  194.2 8.0 reshape.343
  202.1 17.5 all-to-all-start.2
  222.9 4.5 copy.185
  227.4 8.0 reshape.347
  238.3 14.5 all-to-all-start.4
  255.0 5.3 reshape.350
  266.5 118.1 %all-reduce = (f32[32,64]{1,0:T(8,128)S(1)}, f32[64,64]{1,0:T(8,128)S(1)}) all-reduce(f32[32,64]{1,0:T(8,128)S(1)} %fusion.121, f32[64,64]{1,0:T(8,128)S(1)} %fusion.147), channel_id=1, replica_groups=mesh['seq'=64,'chan'=4,'dp'=2] {'seq','chan','dp'}, use_global_device_ids=true, to_apply=%region_11.12 | all-reduce | flops 6144 | bytes 49152 | tf_op jit(solution)/shard_map/psum | solution.py:217
  389.6 6.9 reshape.344
  396.5 4.5 copy.179
  407.0 6.9 reshape.348
  414.0 4.5 copy.187
  425.2 4.5 collective-permute-done.1
  433.1 1438.2 %all-reduce.4.cloned.1.call-done = (f32[3,7,1024]{2,0,1:T(4,128)}, f32[64,1024]{1,0:T(8,128)}) async-done(((f32[3,7,1024]{2,0,1:T(4,128)}, f32[64,1024]{1,0:T(8,128)}), (f32[3,7,1024]{2,0,1:T(4,128)}, f32[64,1024]{1,0:T(8,128)})) %all-reduce.4.cloned.1.call-update) | async-done | bytes 348176 | tf_op jit(solution)/shard_map/psum | solution.py:206
  (171 shorter events, 98.5 us)
Async XLA Ops:
  7.2 9.4 copy-start
  8.3 33.8 %collective-permute-start = (f32[3,2,6,1024]{3,1,2,0:T(2,128)S(1)}, f32[3,2,6,1024]{3,1,2,0:T(2,128)S(1)}, u32[]{:S(2)}, u32[]{:S(2)}) collective-permute-start(f32[3,2,6,1024]{3,1,2,0:T(2,128)S(1)} %copy.198), channel_id=1, source_target_pairs={{0,8},{8,16},{16,24},{24,32},{32,40},{40,48},{48,56},{56,64},{64,7... | collective-permute-start | bytes 442376 | tf_op jit(solution)/shard_map/ppermute | solution.py:14
  12.4 4.9 copy-start.32
  13.1 4.2 copy-start.30
  13.1 4.2 copy-start.31
  13.2 3.3 copy-start.28
  13.2 3.3 copy-start.29
  16.9 25.0 %copy-start.27 = (f32[3,7,1024]{2,1,0:T(8,128)S(1)}, f32[3,7,1024]{2,1,0:T(8,128)}, u32[]{:S(2)}) copy-start(f32[3,7,1024]{2,1,0:T(8,128)} %param.8) | copy-start | bytes 258052
  17.2 24.9 %copy-start.1 = (f32[3,2,64,1024]{3,2,1,0:T(8,128)S(1)}, f32[3,2,64,1024]{3,2,1,0:T(8,128)}, u32[]{:S(2)}) copy-start(f32[3,2,64,1024]{3,2,1,0:T(8,128)} %param.7) | copy-start | bytes 4718596
  20.8 38.4 %all-to-all-start.1 = ((f32[64,1,1024]{2,1,0:T(1,128)}), f32[64,1,1024]{2,1,0:T(1,128)}, u32[]{:S(2)}, u32[]{:S(2)}) async-start(f32[64,1,1024]{2,1,0:T(1,128)} %reshape.341), calls=%async_computation.1 | async-start | bytes 524288 | tf_op jit(solution)/shard_map/all_to_all | solution.py:176
  42.0 1.7 copy-start.14
  59.1 33.6 %all-to-all-start.3 = ((f32[64,1,2048]{2,1,0:T(1,128)}), f32[64,1,2048]{2,1,0:T(1,128)}, u32[]{:S(2)}, u32[]{:S(2)}) async-start(f32[64,1,2048]{2,1,0:T(1,128)} %reshape.345), calls=%async_computation.3 | async-start | bytes 1048576 | tf_op jit(solution)/shard_map/all_to_all | solution.py:181
  92.7 30.4 %all-to-all-start = ((f32[64,1,2048]{2,1,0:T(1,128)}), f32[64,1,2048]{2,1,0:T(1,128)}, u32[]{:S(2)}, u32[]{:S(2)}) async-start(f32[64,1,2048]{2,1,0:T(1,128)} %reshape.339), calls=%async_computation | async-start | bytes 1048576 | tf_op jit(solution)/shard_map/all_to_all | solution.py:178
  130.0 2.9 copy-start.8
  137.6 2.0 copy-start.6
  137.6 2.0 copy-start.7
  169.2 32.9 %all-to-all-start.5 = ((f32[64,1,1024]{2,1,0:T(1,128)}), f32[64,1,1024]{2,1,0:T(1,128)}, u32[]{:S(2)}, u32[]{:S(2)}) async-start(f32[64,1,1024]{2,1,0:T(1,128)} %reshape.349), calls=%async_computation.5 | async-start | bytes 524288 | tf_op jit(solution)/shard_map/all_to_all | solution.py:198
  182.7 3.5 copy-start.3
  202.1 36.1 %all-to-all-start.2 = ((f32[64,1,2048]{2,1,0:T(1,128)}), f32[64,1,2048]{2,1,0:T(1,128)S(1)}, u32[]{:S(2)}, u32[]{:S(2)}) async-start(f32[64,1,2048]{2,1,0:T(1,128)} %reshape.343), calls=%async_computation.2 | async-start | bytes 1048576 | tf_op jit(solution)/shard_map/all_to_all | solution.py:180
  238.3 165.8 %all-to-all-start.4 = ((f32[64,1,2048]{2,1,0:T(1,128)}), f32[64,1,2048]{2,1,0:T(1,128)}, u32[]{:S(2)}, u32[]{:S(2)}) async-start(f32[64,1,2048]{2,1,0:T(1,128)} %reshape.347), calls=%async_computation.4 | async-start | bytes 1048576 | tf_op jit(solution)/shard_map/all_to_all | solution.py:183
  252.8 1618.5 %all-reduce.4.cloned.1.call-start = ((), (), s32[]{:S(2)}) async-start(), calls=%async_computation.6 | async-start | bytes 753664 | tf_op jit(solution)/shard_map/psum | solution.py:206
  262.6 1.8 copy-start.26
  262.6 3.6 copy-start.12
  423.2 6.6 collective-permute-start.1
  (18 other events, 22.2 us)
Sparse Core Ops, SparseCore 0:
  425.4 1445.8 all-reduce.3
where the time goes:
time: 1890 us; the launch traced here: 1880 us
  waiting for transfers between devices  1480 us (78%)
  blocking collectives  118 us (6%)
  starting transfers between devices  95.6 us (5%)
  local copies, waits for them, and re-layouts  80.8 us (4%)
  other arithmetic  58.7 us (3%)
  matrix products  31.1 us (2%)
    psum x1, waiting for transfers between devices, shards(): short_total, out_total = lax.psum((short_local, out_part), ('seq', 'dp'))  1440 us
    psum x1, blocking collectives, shards(): lax.psum((first_part, second_part), ('seq', 'chan', 'dp'))  118 us
    unnamed x90, local copies, waits for them, and re-layouts  49.7 us
  transfers between devices with their start and end apart: 9, of which 6 were waited for; matrix products, arithmetic and copies ran while one was open for 5% of the time, Pallas kernels for 0%

commit v1 on v0

v1 whole, which is shorter than its diff:
```python
import functools
import math

import jax
import jax.numpy as jnp
import ml_dtypes
import numpy as np
from jax import lax
from jax.experimental import pallas as pl
from jax.experimental.pallas import tpu as pltpu
from jax.sharding import PartitionSpec as P

MESH = pl.DeviceIdType.MESH
ROWS = 64
OWN = 16
LANES = 128
SEQ = ROWS * ROWS
RIM = 6
STEP = 512
FLOAT = jnp.float32
HALF = jnp.bfloat16


def halves(table):
    high = table.astype(ml_dtypes.bfloat16)
    low = (table - high.astype(np.float64)).astype(ml_dtypes.bfloat16)
    return high, low


@functools.cache
def tables():
    k = np.arange(ROWS)[:, None] + 0.25
    s = np.arange(ROWS)[None, :]
    theta = 2 * np.pi * k * s / ROWS
    first = np.concatenate([np.cos(theta), -np.sin(theta)], axis=0)
    high, low = halves(first)
    first_stack = np.concatenate([high, high, low], axis=1)
    last = np.concatenate([np.cos(theta).T, -np.sin(theta).T], axis=1) / SEQ
    high, low = halves(last)
    last_stack = np.concatenate([high, high, low], axis=1)
    phi = 2 * np.pi * k * s / SEQ
    turn = np.stack([np.tile(np.cos(phi), (1, 2)), np.tile(np.sin(phi), (1, 2))]).astype(np.float32)
    inner = 2 * np.pi * (np.arange(ROWS)[:, None] * s % ROWS) / ROWS
    cos, sin = np.kron(np.eye(2), np.cos(inner)), np.kron(np.eye(2), np.sin(inner))
    there = np.block([[cos, -sin], [sin, cos]])
    back = np.block([[cos, sin], [-sin, cos]])
    middle = np.stack(halves(there) + halves(back))
    half = 16
    orders = np.arange(half, dtype=np.int64)
    factors = 1 + (SEQ // 2 - 2) * orders * orders // max((half - 1) ** 2, 1)
    angle = 2 * np.pi * (factors[:, None] * np.arange(SEQ)[None, :] % SEQ) / SEQ
    embedded = np.concatenate([np.cos(angle), np.sin(angle)], axis=0).astype(np.float32)
    return first_stack, last_stack, turn, middle, embedded


def split(value):
    high = value.astype(HALF)
    return high, (value - high.astype(FLOAT)).astype(HALF)


def dot(a, b, kind="nn"):
    dims = {"nn": ((1,), (0,)), "nt": ((1,), (1,))}[kind]
    return lax.dot_general(a, b, (dims, ((), ())), preferred_element_type=FLOAT)


def dot3(a, b, kind="nn"):
    ah, al = split(a)
    bh, bl = split(b)
    return dot(ah, bh, kind) + (dot(ah, bl, kind) + dot(al, bh, kind))


def sin_cos(x):
    n = jnp.floor(x * (2.0 / math.pi) + 0.5)
    r = x - n * 1.5703125
    r = r - n * 4.837512969970703125e-4
    r = r - n * 7.549789948768648e-8
    z = r * r
    s = r + r * z * (-1.6666654611e-1 + z * (8.3321608736e-3 + z * -1.9515295891e-4))
    c = 1.0 - 0.5 * z + z * z * (4.166664568298827e-2 + z * (-1.388731625493765e-3 + z * 2.443315711809948e-5))
    q = n.astype(jnp.int32)
    odd = (q & 1) == 1
    sin = jnp.where(odd, c, s)
    cos = jnp.where(odd, s, c)
    sin = jnp.where((q & 2) == 2, -sin, sin)
    cos = jnp.where(((q + 1) & 2) == 2, -cos, cos)
    return sin, cos


def exchange_kernel(same, x_ref, o_ref, send_sem, recv_sem, here_sem):
    me = lax.axis_index("seq")
    barrier = pltpu.get_barrier_semaphore()

    def greet(i, carry):
        pl.semaphore_signal(
            barrier, inc=1, device_id={"seq": lax.rem(me + i, ROWS)}, device_id_type=MESH
        )
        return carry

    lax.fori_loop(1, ROWS, greet, 0)
    pl.semaphore_wait(barrier, ROWS - 1)
    block = (lambda i: x_ref) if same else (lambda i: x_ref.at[i])
    here = pltpu.make_async_copy(block(me), o_ref.at[me], here_sem)
    here.start()

    def send(i, carry):
        z = lax.rem(me // 16 + lax.rem(i, 4), 4)
        x = lax.rem(lax.rem(me // 4, 4) + lax.rem(i // 4, 4), 4)
        y = lax.rem(lax.rem(me, 4) + i // 16, 4)
        peer = z * 16 + x * 4 + y
        pltpu.make_async_remote_copy(
            src_ref=block(peer),
            dst_ref=o_ref.at[me],
            send_sem=send_sem,
            recv_sem=recv_sem,
            device_id={"seq": peer},
            device_id_type=MESH,
        ).start()
        return carry

    lax.fori_loop(1, ROWS, send, 0)
    here.wait()
    pltpu.make_async_remote_copy(
        src_ref=o_ref.at[pl.ds(0, ROWS - 1)],
        dst_ref=o_ref.at[pl.ds(0, ROWS - 1)],
        send_sem=send_sem,
        recv_sem=recv_sem,
        device_id={"seq": me},
        device_id_type=MESH,
    ).wait()


def exchange(value, collective_id, same=False):
    shape = (ROWS,) + value.shape if same else value.shape
    return pl.pallas_call(
        functools.partial(exchange_kernel, same),
        out_shape=jax.ShapeDtypeStruct(shape, FLOAT),
        in_specs=[pl.BlockSpec(memory_space=pl.ANY)],
        out_specs=pl.BlockSpec(memory_space=pl.ANY),
        scratch_shapes=[pltpu.SemaphoreType.DMA] * 3,
        compiler_params=pltpu.CompilerParams(collective_id=collective_id, has_side_effects=True),
        name="exchange%d" % collective_id,
    )(value)


def feature_kernel(proj_ref, rim_ref, taps_ref, cot_ref, feat_ref, send_ref, ext):
    ext[:, :, :8, :] = rim_ref[...]
    ext[:, :, 8:, :] = proj_ref[...]
    feats = [[None, None] for _ in range(3)]
    for i in range(3):
        for w in range(2):
            total = taps_ref[i, 0:1, :] * ext[i, w, 8:, :]
            for j in range(1, RIM + 1):
                total = total + taps_ref[i, j : j + 1, :] * ext[i, w, 8 - j : 8 - j + ROWS, :]
            feats[i][w] = total
            feat_ref[i, w] = total
    product = jnp.concatenate([feats[1][w] * feats[2][w] for w in range(2)], axis=0)
    grad = jnp.concatenate([cot_ref[w] * feats[0][w] for w in range(2)], axis=0)
    send_ref[:, :OWN, :] = product.T.reshape(8, OWN, LANES)
    send_ref[:, OWN:, :] = grad.T.reshape(8, OWN, LANES)


def by_channels(shape, size=LANES):
    block = shape[:-1] + (size,)
    lead = len(shape) - 1
    return pl.BlockSpec(block, lambda c: (0,) * lead + (c,))


def features(projected, rim, taps, cotangent):
    blocks = projected.shape[-1] // LANES
    return pl.pallas_call(
        feature_kernel,
        grid=(blocks,),
        out_shape=(
            jax.ShapeDtypeStruct(projected.shape, FLOAT),
            jax.ShapeDtypeStruct((ROWS, 2 * OWN, LANES), FLOAT),
        ),
        in_specs=[by_channels(v.shape) for v in (projected, rim, taps, cotangent)],
        out_specs=(
            by_channels(projected.shape),
            pl.BlockSpec((8, 2 * OWN, LANES), lambda c: (c, 0, 0)),
        ),
        scratch_shapes=[pltpu.VMEM((3, 2, ROWS + 8, LANES), FLOAT)],
        name="features",
    )(projected, rim, taps, cotangent)


def owner_kernel(
    scale_ref,
    got_ref,
    emb_ref,
    w1t_ref,
    w2t_ref,
    w2_ref,
    wot_ref,
    wo_ref,
    first_ref,
    last_ref,
    turn_ref,
    middle_ref,
    back_ref,
    out_ref,
    net_ref,
    act1,
    cos1,
    act2,
    cos2,
    filt,
    fgrad,
):
    lane = lax.broadcasted_iota(jnp.int32, (OWN, LANES), 1)
    low_half = lane < ROWS

    def net(step, carry):
        cols = pl.ds(pl.multiple_of(step * STEP, STEP), STEP)
        pre1 = dot3(w1t_ref[...], emb_ref[:, cols])
        s1, c1 = sin_cos(pre1)
        act1[:, cols] = s1
        cos1[:, cols] = c1
        pre2 = dot3(w2t_ref[...], s1)
        s2, c2 = sin_cos(pre2)
        act2[:, cols] = s2
        cos2[:, cols] = c2
        raw = dot3(wot_ref[...], s2)
        for pair in range(STEP // LANES):
            both = raw[:, pair * LANES : (pair + 1) * LANES]
            turned = pltpu.roll(both, ROWS, 1)
            base = pl.multiple_of((step * (STEP // ROWS) + 2 * pair) * OWN, OWN)
            filt[pl.ds(base, OWN), :] = jnp.where(low_half, both, turned)
            filt[pl.ds(base + OWN, OWN), :] = jnp.where(low_half, turned, both)
        return carry

    lax.fori_loop(0, SEQ // STEP, net, 0)

    place = lax.broadcasted_iota(jnp.int32, (ROWS, LANES), 0) * ROWS + (
        lax.broadcasted_iota(jnp.int32, (ROWS, LANES), 1) & (ROWS - 1)
    )
    place = place.astype(FLOAT)

    def channel(ch, carry):
        cos, sin = turn_ref[0], turn_ref[1]
        envelope = jnp.exp(place * -scale_ref[0, ch]) * scale_ref[1, ch]
        prod = got_ref[pl.ds(ch, ROWS, stride=2 * OWN), :]
        grad = got_ref[pl.ds(ch + OWN, ROWS, stride=2 * OWN), :]
        kern = filt[pl.ds(ch, ROWS, stride=OWN), :] * envelope
        high, low = split(jnp.concatenate([prod, grad, kern], axis=1))
        spec = dot(first_ref[...], jnp.concatenate([high, low, high], axis=0))
        rows = []
        for i in range(3):
            re = spec[:ROWS, i * LANES : (i + 1) * LANES]
            im = spec[ROWS:, i * LANES : (i + 1) * LANES]
            rows.append(jnp.concatenate([re * cos + im * sin, im * cos - re * sin], axis=1))
        high, low = split(jnp.concatenate(rows, axis=0))
        freq = dot(high, middle_ref[0]) + (dot(low, middle_ref[0]) + dot(high, middle_ref[1]))
        pr, pi = freq[:ROWS, :LANES], freq[:ROWS, LANES:]
        gr, gi = freq[ROWS : 2 * ROWS, :LANES], freq[ROWS : 2 * ROWS, LANES:]
        kr, ki = freq[2 * ROWS :, :LANES], freq[2 * ROWS :, LANES:]
        cr, ci = pr * gr + pi * gi, pr * gi - pi * gr
        cr, ci = cr + pltpu.roll(cr, ROWS, 1), ci + pltpu.roll(ci, ROWS, 1)
        rows = [
            jnp.concatenate([pr * kr - pi * ki, pr * ki + pi * kr], axis=1),
            jnp.concatenate([kr * gr + ki * gi, kr * gi - ki * gr], axis=1),
            jnp.concatenate([cr, ci], axis=1),
        ]
        high, low = split(jnp.concatenate(rows, axis=0))
        freq = dot(high, middle_ref[2]) + (dot(low, middle_ref[2]) + dot(high, middle_ref[3]))
        cols = []
        for i in range(3):
            re = freq[i * ROWS : (i + 1) * ROWS, :LANES]
            im = freq[i * ROWS : (i + 1) * ROWS, LANES:]
            cols.append(jnp.concatenate([re * cos - im * sin, re * sin + im * cos], axis=0))
        high, low = split(jnp.concatenate(cols, axis=1))
        time = dot(last_ref[...], jnp.concatenate([high, low, high], axis=0))
        back_ref[pl.ds(ch, ROWS, stride=2 * OWN), :] = time[:, :LANES]
        back_ref[pl.ds(ch + OWN, ROWS, stride=2 * OWN), :] = time[:, LANES : 2 * LANES]
        fgrad[pl.ds(ch, ROWS, stride=OWN), :] = time[:, 2 * LANES :] * envelope
        return carry

    lax.fori_loop(0, OWN, channel, 0)

    out_ref[...] = jnp.zeros_like(out_ref)
    net_ref[...] = jnp.zeros_like(net_ref)

    def net_back(step, carry):
        cols = pl.ds(pl.multiple_of(step * STEP, STEP), STEP)
        parts = []
        for pair in range(STEP // LANES):
            base = pl.multiple_of((step * (STEP // ROWS) + 2 * pair) * OWN, OWN)
            parts.append(
                jnp.where(low_half, fgrad[pl.ds(base, OWN), :], fgrad[pl.ds(base + OWN, OWN), :])
            )
        kgrad = jnp.concatenate(parts, axis=1)
        out_ref[...] += dot3(kgrad, act2[:, cols], "nt")
        pre2 = dot3(wo_ref[...], kgrad) * cos2[:, cols]
        net_ref[32:, :] += dot3(act1[:, cols], pre2, "nt")
        pre1 = dot3(w2_ref[...], pre2) * cos1[:, cols]
        net_ref[:32, :] += dot3(emb_ref[:, cols], pre1, "nt")
        return carry

    lax.fori_loop(0, SEQ // STEP, net_back, 0)


def owner(scale, got, w1, w2, wo):
    first_stack, last_stack, turn, middle, embedded = tables()
    vmem = pl.BlockSpec(memory_space=pltpu.VMEM)
    hidden = w2.shape[0]
    return pl.pallas_call(
        owner_kernel,
        out_shape=(
            jax.ShapeDtypeStruct((ROWS * 2 * OWN, LANES), FLOAT),
            jax.ShapeDtypeStruct((OWN, hidden), FLOAT),
            jax.ShapeDtypeStruct((w1.shape[0] + hidden, hidden), FLOAT),
        ),
        in_specs=[pl.BlockSpec(memory_space=pltpu.SMEM)] + [vmem] * 11,
        out_specs=(vmem, vmem, vmem),
        scratch_shapes=[pltpu.VMEM((hidden, SEQ), FLOAT)] * 4
        + [pltpu.VMEM((ROWS * OWN, LANES), FLOAT)] * 2,
        compiler_params=pltpu.CompilerParams(vmem_limit_bytes=40 << 20),
        name="owner",
    )(
        scale,
        got.reshape(ROWS * 2 * OWN, LANES),
        jnp.asarray(embedded),
        w1.T,
        w2.T,
        w2,
        wo.T,
        wo,
        jnp.asarray(first_stack),
        jnp.asarray(last_stack),
        jnp.asarray(turn),
        jnp.asarray(middle),
    )


def mix_kernel(feat_ref, cot_ref, got_ref, mixed_ref, grad_ref):
    conv = got_ref[:, :OWN, :].reshape(LANES, LANES).T
    back = got_ref[:, OWN:, :].reshape(LANES, LANES).T
    for w in range(2):
        rows = slice(w * ROWS, (w + 1) * ROWS)
        mixed_ref[w] = feat_ref[0, w] * conv[rows]
        grad_ref[0, w] = cot_ref[w] * conv[rows]
        grad_ref[1, w] = back[rows] * feat_ref[2, w]
        grad_ref[2, w] = back[rows] * feat_ref[1, w]


def mix(feat, cotangent, got):
    return pl.pallas_call(
        mix_kernel,
        grid=(feat.shape[-1] // LANES,),
        out_shape=(
            jax.ShapeDtypeStruct(cotangent.shape, FLOAT),
            jax.ShapeDtypeStruct(feat.shape, FLOAT),
        ),
        in_specs=[
            by_channels(feat.shape),
            by_channels(cotangent.shape),
            pl.BlockSpec((8, 2 * OWN, LANES), lambda c: (c, 0, 0)),
        ],
        out_specs=(by_channels(cotangent.shape), by_channels(feat.shape)),
        name="mix",
    )(feat, cotangent, got)


def taps_kernel(grad_ref, next_ref, proj_ref, rim_ref, taps_ref, raw_ref, short_ref, ext, ahead):
    ext[:, :, :8, :] = rim_ref[...]
    ext[:, :, 8:, :] = proj_ref[...]
    ahead[:, :, :ROWS, :] = grad_ref[...]
    ahead[:, :, ROWS:, :] = next_ref[...]
    for i in range(3):
        for w in range(2):
            total = taps_ref[i, 0:1, :] * grad_ref[i, w]
            for j in range(1, RIM + 1):
                total = total + taps_ref[i, j : j + 1, :] * ahead[i, w, j : j + ROWS, :]
            raw_ref[i, w] = total
        for j in range(RIM + 1):
            both = grad_ref[i, 0] * ext[i, 0, 8 - j : 8 - j + ROWS, :]
            both = both + grad_ref[i, 1] * ext[i, 1, 8 - j : 8 - j + ROWS, :]
            short_ref[i, j : j + 1, :] = jnp.sum(both, axis=0, keepdims=True)


def tap_grads(grad, following, projected, rim, taps):
    args = (grad, following, projected, rim, taps)
    return pl.pallas_call(
        taps_kernel,
        grid=(grad.shape[-1] // LANES,),
        out_shape=(
            jax.ShapeDtypeStruct(grad.shape, FLOAT),
            jax.ShapeDtypeStruct(taps.shape, FLOAT),
        ),
        in_specs=[by_channels(v.shape) for v in args],
        out_specs=(by_channels(grad.shape), by_channels(taps.shape)),
        scratch_shapes=[pltpu.VMEM((3, 2, ROWS + 8, LANES), FLOAT)] * 2,
        name="taps",
    )(*args)


def swapped(value, axis, bit):
    count = lax.axis_size(axis)
    return lax.ppermute(value, axis, [(i, i ^ bit) for i in range(count)])


def shards(projected, short_weight, decay_rates, w1, w2, out_weight, cotangent):
    place = lax.axis_index("seq")
    group = projected.shape[-1]
    rim = lax.ppermute(
        projected[:, :, ROWS - 8 :, :], "seq", [(i, i + 1) for i in range(ROWS - 1)]
    )
    feat, sends = features(projected, rim, short_weight, cotangent)
    got = exchange(sends, 1)
    rates = lax.dynamic_slice_in_dim(decay_rates, place * OWN, OWN, 0)
    wo = lax.dynamic_slice_in_dim(out_weight, place * OWN, OWN, 1)
    scale = jnp.stack([rates, jnp.sqrt(2.0 * rates + 1.0 / SEQ)])
    back, out_part, net_part = owner(scale, got, w1, w2, wo)
    back_got = exchange(back.reshape(ROWS, 2 * OWN, LANES), 2)
    small = jnp.concatenate([out_part, net_part], axis=0)
    small = small + swapped(small, "dp", 1)
    out_own, net_sum = small[:OWN], small[OWN:]
    net_sum = net_sum + swapped(net_sum, "chan", 1)
    net_sum = net_sum + swapped(net_sum, "chan", 2)
    mixed, grad = mix(feat, cotangent, back_got)
    following = lax.ppermute(
        grad[:, :, :8, :], "seq", [(i + 1, i) for i in range(ROWS - 1)]
    )
    raw, short = tap_grads(grad, following, projected, rim, short_weight)
    short = short + swapped(short, "dp", 1)
    tap_count = short.shape[0] * short.shape[1]
    pieces = jnp.concatenate(
        [
            jnp.moveaxis(short.reshape(tap_count, ROWS, OWN), 1, 0).reshape(ROWS, tap_count * OWN),
            net_sum.reshape(ROWS, -1),
        ],
        axis=1,
    )
    width = 4 * LANES
    pieces = jnp.pad(pieces, ((0, 0), (0, 2 * width - pieces.shape[1]))).reshape(ROWS, 8, LANES)
    summed = jnp.sum(exchange(pieces, 3), axis=0)
    every = exchange(jnp.concatenate([summed, out_own.reshape(8, LANES)], axis=0), 4, same=True)
    flat = every[:, :4].reshape(ROWS, width)
    short_total = jnp.moveaxis(flat[:, : tap_count * OWN].reshape(ROWS, tap_count, OWN), 0, 1)
    short_total = short_total.reshape(short.shape)
    net_total = flat[:, tap_count * OWN : tap_count * OWN + net_sum.size // ROWS]
    net_total = net_total.reshape(net_sum.shape)
    out_total = every[:, 8:].reshape(group, -1).T
    windows = projected.shape[1] * lax.axis_size("dp")
    tail = 1.0 / math.sqrt(windows * SEQ)
    scale = 4.0 / math.sqrt(windows * SEQ * group * lax.axis_size("chan"))
    split_at = w1.shape[0]
    return (
        mixed,
        raw,
        short_total * tail,
        out_total * tail,
        net_total[:split_at] * scale,
        net_total[split_at:] * scale,
    )


def solution(mesh):
    return jax.shard_map(
        shards,
        mesh=mesh,
        in_specs=(
            P(None, "dp", "seq", "chan"),
            P(None, None, "chan"),
            P("chan"),
            P(),
            P(),
            P(None, "chan"),
            P("dp", "seq", "chan"),
        ),
        out_specs=(
            P("dp", "seq", "chan"),
            P(None, "dp", "seq", "chan"),
            P(None, None, "chan"),
            P(None, "chan"),
            P(),
            P(),
        ),
        check_vma=False,
    )
```

time: 1890 us -> 291 us (0.15)
  waiting for transfers between devices: 1480 us -> 4.53 us
  Pallas kernels: 0 us -> 237 us
  blocking collectives: 118 us -> 0 us
  local copies, waits for them, and re-layouts: 80.8 us -> 12.5 us
  starting transfers between devices: 95.6 us -> 27.6 us
  other arithmetic: 58.7 us -> 5.6 us
  matrix products: 31.1 us -> 0 us
    psum x1 -> x0, waiting for transfers between devices: 1440 us -> none  [shards(): short_total, out_total = lax.psum((short_local, out_part), ('seq', 'dp'))]
    pallas_call x0 -> x8, Pallas kernels: none -> 237 us  [the longest x4 190 us: exchange(): pl.pallas_call(functools.partial(exchange_kernel, same), out_shape=jax.Sh...]
    psum x1 -> x0, blocking collectives: 118 us -> none  [shards(): lax.psum((first_part, second_part), ('seq', 'chan', 'dp'))]
    all_to_all x6 -> x0, starting transfers between devices: 90.2 us -> none  [the longest x1 21.1 us: shards(): lax.all_to_all(kernel, 'seq', split_axis=2, concat_axis=1, tiled=True)]
    unnamed x90 -> x28, local copies, waits for them, and re-layouts: 49.7 us -> 6.24 us
    all_to_all x6 -> x0, waiting for transfers between devices: 39.3 us -> none  [the longest x1 19.6 us: shards(): lax.all_to_all(grad_conv, 'seq', split_axis=2, concat_axis=1, tiled=True)]
    dot_general x20 -> x0, matrix products: 31.1 us -> none  [the longest x3 6.27 us: restore(): jnp.einsum('rbckj,rsjm->sbckm', freq, inverse_second, precision=precise)]
    ppermute x2 -> x6, starting transfers between devices: 5.33 us -> 27.6 us  [the longest x4 22.3 us: swapped(): return lax.ppermute(value, axis, [(i, i ^ bit) for i in range(count)])]
  transfers between devices with their start and end apart: 9 -> 6, of which waited for: 6 -> 3; matrix products, arithmetic and copies ran while one was open for 5% -> 1% of each run, Pallas kernels for 0% -> 2%
where the time goes in v1:
time: 291 us; the launch traced here: 289 us
  Pallas kernels  237 us (81%)
  starting transfers between devices  27.6 us (9%)
  local copies, waits for them, and re-layouts  12.5 us (4%)
  other arithmetic  5.6 us (2%)
  waiting for transfers between devices  4.53 us (2%)
    pallas_call x4, Pallas kernels, exchange(): pl.pallas_call(functools.partial(exchange_kernel, same), out_shape=jax.Sh...  190 us
    pallas_call x1, Pallas kernels, owner(): pl.pallas_call(owner_kernel, out_shape=(jax.ShapeDtypeStruct((ROWS * 2 *...  28.5 us
    ppermute x4, starting transfers between devices, swapped(): return lax.ppermute(value, axis, [(i, i ^ bit) for i in range(count)])  22.3 us
    pallas_call x1, Pallas kernels, tap_grads(): pl.pallas_call(taps_kernel, grid=(grad.shape[-1] // LANES,), out_shape=(j...  6.69 us
    pallas_call x1, Pallas kernels, mix(): pl.pallas_call(mix_kernel, grid=(feat.shape[-1] // LANES,), out_shape=(ja...  6.42 us
    unnamed x28, local copies, waits for them, and re-layouts  6.24 us
    pallas_call x1, Pallas kernels, features(): pl.pallas_call(feature_kernel, grid=(blocks,), out_shape=(jax.ShapeDtypeS...  6.18 us
  transfers between devices with their start and end apart: 6, of which 3 were waited for; matrix products, arithmetic and copies ran while one was open for 1% of the time, Pallas kernels for 2%

profile of v1, /device:TPU:1, one launch (start us, length us, event | category | flops | bytes accessed | tf_op | source)
XLA Modules:
  0.0 288.7 jit_solution(18072606472179629892)
XLA Ops:
  0.6 1.0 slice.30
  1.6 4.0 %collective-permute-start = (f32[3,2,8,1024]{3,2,1,0:T(8,128)S(1)}, f32[3,2,8,1024]{3,2,1,0:T(8,128)S(1)}, u32[]{:S(2)}, u32[]{:S(2)}) collective-permute-start(f32[3,2,8,1024]{3,2,1,0:T(8,128)S(1)} %slice.30), channel_id=1, source_target_pairs={{0,8},{8,16},{16,24},{24,32},{32,40},{40,48},{48,56},{56,64},{64,7... | collective-permute-start | bytes 589832 | tf_op jit(solution)/shard_map/ppermute | solution.py:405
  9.0 6.2 %features.1 = (f32[3,2,64,1024]{3,2,1,0:T(8,128)}, f32[64,32,128]{2,1,0:T(8,128)}) custom-call(f32[3,2,64,1024]{3,2,1,0:T(8,128)} %proj_ref.3, f32[3,2,8,1024]{3,2,1,0:T(8,128)} %copy-done.9, f32[3,7,1024]{2,1,0:T(8,128)} %taps_ref.3, f32[2,64,1024]{2,1,0:T(8,128)} %cot_ref.3), custom_call_target="tpu_custom_call" | custom-call | tf_op jit(solution)/shard_map/features/pallas_call | solution.py:170
  15.3 84.1 %exchange1.1 = f32[64,32,128]{2,1,0:T(8,128)} custom-call(f32[64,32,128]{2,1,0:T(8,128)} %get-tuple-element.16.x_ref), custom_call_target="tpu_custom_call" | custom-call | tf_op jit(solution)/shard_map/exchange1/pallas_call | solution.py:134
  99.5 1.2 copy-done.1
  100.7 28.5 %owner.1 = (f32[2048,128]{1,0:T(8,128)S(1)}, f32[16,64]{1,0:T(8,128)S(1)}, f32[96,64]{1,0:T(8,128)S(1)}) custom-call(f32[2,16]{1,0:T(2,128)S(1)} %pad_maximum_fusion.1.scale_ref, f32[2048,128]{1,0:T(8,128)S(1)} %bitcast.21, f32[32,4096]{1,0:T(8,128)S(1)} %copy-done.4, f32[64,32]{1,0:T(8,128)S(1)} %bitcast.23, f32[64,64]{1,0:T(8,128)S(1)} %bitcast.24, ...), custom_call_target="tpu_custom_call" | custom-call | tf_op jit(solution)/shard_map/owner/pallas_call | solution.py:306
  129.2 1.0 copy-done.2
  130.1 38.2 %exchange2.1.got_ref = f32[64,32,128]{2,1,0:T(8,128)} custom-call(f32[64,32,128]{2,1,0:T(8,128)} %bitcast.22), custom_call_target="tpu_custom_call" | custom-call | tf_op jit(solution)/shard_map/exchange2/pallas_call | solution.py:134
  168.3 6.4 %mix.1 = (f32[2,64,1024]{2,1,0:T(8,128)}, f32[3,2,64,1024]{3,2,1,0:T(8,128)}) custom-call(f32[3,2,64,1024]{3,2,1,0:T(8,128)} %get-tuple-element.15.feat_ref, f32[2,64,1024]{2,1,0:T(8,128)} %cot_ref.3, f32[64,32,128]{2,1,0:T(8,128)} %exchange2.1.got_ref), custom_call_target="tpu_custom_call" | custom-call | tf_op jit(solution)/shard_map/mix/pallas_call | solution.py:347
  174.7 0.9 slice.31
  175.7 1.3 collective-permute-start.1
  177.0 2.5 collective-permute-start.3
  180.4 1.9 collective-permute-start.4
  182.3 1.1 collective-permute-done.1.next_ref
  184.1 6.7 %taps.1 = (f32[3,2,64,1024]{3,2,1,0:T(8,128)}, f32[3,7,1024]{2,1,0:T(8,128)}) custom-call(f32[3,2,64,1024]{3,2,1,0:T(8,128)} %get-tuple-element.19.grad_ref, f32[3,2,8,1024]{3,2,1,0:T(8,128)} %copy-done.10, f32[3,2,64,1024]{3,2,1,0:T(8,128)} %proj_ref.3, f32[3,2,8,1024]{3,2,1,0:T(8,128)} %copy-done.9, f32[3,7,1024]{2,1,0:T(8,128)} %taps_ref.3), custom_call_target="tpu_custom_call" | custom-call | tf_op jit(solution)/shard_map/taps/pallas_call | solution.py:383
  190.8 3.3 %collective-permute-start.2 = (f32[3,7,1024]{2,1,0:T(8,128)}, f32[3,7,1024]{2,1,0:T(8,128)S(1)}, u32[]{:S(2)}, u32[]{:S(2)}) collective-permute-start(f32[3,7,1024]{2,1,0:T(8,128)} %get-tuple-element.21), channel_id=1, source_target_pairs={{0,1},{1,0},{2,3},{3,2},{4,5},{5,4},{6,7},{7,6},{8,9},{9,8},{10,11... | collective-permute-start | bytes 258056 | tf_op jit(solution)/shard_map/ppermute | solution.py:399
  194.2 14.5 %collective-permute-start.5 = (f32[96,64]{1,0:T(8,128)S(1)}, f32[96,64]{1,0:T(8,128)S(1)}, u32[]{:S(2)}, u32[]{:S(2)}) collective-permute-start(f32[96,64]{1,0:T(8,128)S(1)} %slice_add_fusion), channel_id=1, source_target_pairs={{0,4},{2,6},{4,0},{6,2},{1,5},{3,7},{5,1},{7,3},{8,12},{10,14},{12... | collective-permute-start | bytes 73736 | tf_op jit(solution)/shard_map/ppermute | solution.py:399
  208.8 2.5 collective-permute-done.5
  213.9 34.9 %exchange3.1 = f32[64,8,128]{2,1,0:T(8,128)} custom-call(f32[64,8,128]{2,1,0:T(8,128)} %copy.33.x_ref), custom_call_target="tpu_custom_call" | custom-call | tf_op jit(solution)/shard_map/exchange3/pallas_call | solution.py:134
  248.8 1.0 reduce_sum.9
  250.4 32.4 %exchange4.1 = f32[64,16,128]{2,1,0:T(8,128)} custom-call(f32[16,128]{1,0:T(8,128)} %pad_maximum_fusion.x_ref), custom_call_target="tpu_custom_call" | custom-call | tf_op jit(solution)/shard_map/exchange4/pallas_call | solution.py:134
  282.8 1.0 slice.34
  283.8 1.0 slice_multiply_fusion
  287.6 1.0 mul.52
  (58 shorter events, 10.9 us)
Async XLA Ops:
  0.6 7.5 %copy-start = (f32[64,1024]{1,0:T(8,128)S(1)}, f32[64,1024]{1,0:T(8,128)}, u32[]{:S(2)}) copy-start(f32[64,1024]{1,0:T(8,128)} %param.17) | copy-start | bytes 786436
  1.6 6.7 %collective-permute-start = (f32[3,2,8,1024]{3,2,1,0:T(8,128)S(1)}, f32[3,2,8,1024]{3,2,1,0:T(8,128)S(1)}, u32[]{:S(2)}, u32[]{:S(2)}) collective-permute-start(f32[3,2,8,1024]{3,2,1,0:T(8,128)S(1)} %slice.30), channel_id=1, source_target_pairs={{0,8},{8,16},{16,24},{24,32},{32,40},{40,48},{48,56},{56,64},{64,7... | collective-permute-start | bytes 589832 | tf_op jit(solution)/shard_map/ppermute | solution.py:405
  8.3 0.7 copy-start.9
  15.2 84.2 %copy-start.3 = (bf16[4,256,256]{2,1,0:T(8,128)(2,1)S(1)}, bf16[4,256,256]{2,1,0:T(8,128)(2,1)}, u32[]{:S(2)}) copy-start(bf16[4,256,256]{2,1,0:T(8,128)(2,1)} %constant.39.clone.middle_ref) | copy-start | bytes 1572868
  15.2 84.2 %copy-start.4 = (f32[32,4096]{1,0:T(8,128)S(1)}, f32[32,4096]{1,0:T(8,128)}, u32[]{:S(2)}) copy-start(f32[32,4096]{1,0:T(8,128)} %constant.35.clone.emb_ref) | copy-start | bytes 1572868
  15.2 84.2 %copy-start.5 = (f32[64,64]{1,0:T(8,128)S(1)}, f32[64,64]{1,0:T(8,128)}, u32[]{:S(2)}) copy-start(f32[64,64]{1,0:T(8,128)} %w2_ref.1) | copy-start | bytes 49156
  15.2 84.2 %copy-start.6 = (f32[2,64,128]{2,1,0:T(8,128)S(1)}, f32[2,64,128]{2,1,0:T(8,128)}, u32[]{:S(2)}) copy-start(f32[2,64,128]{2,1,0:T(8,128)} %constant.38.clone.turn_ref) | copy-start | bytes 196612
  15.2 84.2 %copy-start.7 = (bf16[128,192]{1,0:T(8,128)(2,1)S(1)}, bf16[128,192]{1,0:T(8,128)(2,1)}, u32[]{:S(2)}) copy-start(bf16[128,192]{1,0:T(8,128)(2,1)} %constant.36.clone.first_ref) | copy-start | bytes 147460
  15.3 84.2 %copy-start.8 = (bf16[64,384]{1,0:T(8,128)(2,1)S(1)}, bf16[64,384]{1,0:T(8,128)(2,1)}, u32[]{:S(2)}) copy-start(bf16[64,384]{1,0:T(8,128)(2,1)} %constant.37.clone.last_ref) | copy-start | bytes 147460
  99.5 1.2 copy-start.1
  129.2 1.0 copy-start.2
  175.7 7.8 %collective-permute-start.1 = (f32[3,2,8,1024]{3,2,1,0:T(8,128)S(1)}, f32[3,2,8,1024]{3,2,1,0:T(8,128)S(1)}, u32[]{:S(2)}, u32[]{:S(2)}) collective-permute-start(f32[3,2,8,1024]{3,2,1,0:T(8,128)S(1)} %slice.31), channel_id=1, source_target_pairs={{8,0},{16,8},{24,16},{32,24},{40,32},{48,40},{56,48},{64,56},{72,6... | collective-permute-start | bytes 589832 | tf_op jit(solution)/shard_map/ppermute | solution.py:421
  177.0 3.4 %collective-permute-start.3 = (f32[112,64]{1,0:T(8,128)S(1)}, f32[112,64]{1,0:T(8,128)S(1)}, u32[]{:S(2)}, u32[]{:S(2)}) collective-permute-start(f32[112,64]{1,0:T(8,128)S(1)} %constant_dynamic-update-slice_fusion), channel_id=1, source_target_pairs={{0,1},{1,0},{2,3},{3,2},{4,5},{5,4},{6,7},{7,6},{8,9},{9,8},{10,11... | collective-permute-start | bytes 86024 | tf_op jit(solution)/shard_map/ppermute | solution.py:399
  180.4 13.8 %collective-permute-start.4 = (f32[96,64]{1,0:T(8,128)S(1)}, f32[96,64]{1,0:T(8,128)S(1)}, u32[]{:S(2)}, u32[]{:S(2)}) collective-permute-start(f32[96,64]{1,0:T(8,128)S(1)} %slice.40), channel_id=1, source_target_pairs={{0,2},{2,0},{4,6},{6,4},{1,3},{3,1},{5,7},{7,5},{8,10},{10,8},{12,... | collective-permute-start | bytes 73736 | tf_op jit(solution)/shard_map/ppermute | solution.py:399
  183.4 0.7 copy-start.10
  190.8 20.7 %collective-permute-start.2 = (f32[3,7,1024]{2,1,0:T(8,128)}, f32[3,7,1024]{2,1,0:T(8,128)S(1)}, u32[]{:S(2)}, u32[]{:S(2)}) collective-permute-start(f32[3,7,1024]{2,1,0:T(8,128)} %get-tuple-element.21), channel_id=1, source_target_pairs={{0,1},{1,0},{2,3},{3,2},{4,5},{5,4},{6,7},{7,6},{8,9},{9,8},{10,11... | collective-permute-start | bytes 258056 | tf_op jit(solution)/shard_map/ppermute | solution.py:399
  194.2 17.1 %collective-permute-start.5 = (f32[96,64]{1,0:T(8,128)S(1)}, f32[96,64]{1,0:T(8,128)S(1)}, u32[]{:S(2)}, u32[]{:S(2)}) collective-permute-start(f32[96,64]{1,0:T(8,128)S(1)} %slice_add_fusion), channel_id=1, source_target_pairs={{0,4},{2,6},{4,0},{6,2},{1,5},{3,7},{5,1},{7,3},{8,12},{10,14},{12... | collective-permute-start | bytes 73736 | tf_op jit(solution)/shard_map/ppermute | solution.py:399

commit v2 on v1

v2 whole, which is shorter than its diff:
```python
import functools
import math

import jax
import jax.numpy as jnp
import ml_dtypes
import numpy as np
from jax import lax
from jax.experimental import pallas as pl
from jax.experimental.pallas import tpu as pltpu
from jax.sharding import PartitionSpec as P

MESH = pl.DeviceIdType.MESH
ROWS = 64
OWN = 16
LANES = 128
SEQ = ROWS * ROWS
RIM = 6
STEP = 512
FLOAT = jnp.float32
HALF = jnp.bfloat16


def halves(table):
    high = table.astype(ml_dtypes.bfloat16)
    low = (table - high.astype(np.float64)).astype(ml_dtypes.bfloat16)
    return high, low


@functools.cache
def tables():
    k = np.arange(ROWS)[:, None] + 0.25
    s = np.arange(ROWS)[None, :]
    theta = 2 * np.pi * k * s / ROWS
    first = np.concatenate([np.cos(theta), -np.sin(theta)], axis=0)
    high, low = halves(first)
    first_stack = np.concatenate([high, high, low], axis=1)
    last = np.concatenate([np.cos(theta).T, -np.sin(theta).T], axis=1) / SEQ
    high, low = halves(last)
    last_stack = np.concatenate([high, high, low], axis=1)
    phi = 2 * np.pi * k * s / SEQ
    turn = np.stack([np.tile(np.cos(phi), (1, 2)), np.tile(np.sin(phi), (1, 2))]).astype(np.float32)
    inner = 2 * np.pi * (np.arange(ROWS)[:, None] * s % ROWS) / ROWS
    cos, sin = np.kron(np.eye(2), np.cos(inner)), np.kron(np.eye(2), np.sin(inner))
    there = np.block([[cos, -sin], [sin, cos]])
    back = np.block([[cos, sin], [-sin, cos]])
    middle = np.stack(halves(there) + halves(back))
    half = 16
    orders = np.arange(half, dtype=np.int64)
    factors = 1 + (SEQ // 2 - 2) * orders * orders // max((half - 1) ** 2, 1)
    angle = 2 * np.pi * (factors[:, None] * np.arange(SEQ)[None, :] % SEQ) / SEQ
    embedded = np.concatenate([np.cos(angle), np.sin(angle)], axis=0).astype(np.float32)
    return first_stack, last_stack, turn, middle, embedded


def split(value):
    high = value.astype(HALF)
    return high, (value - high.astype(FLOAT)).astype(HALF)


def dot(a, b, kind="nn"):
    dims = {"nn": ((1,), (0,)), "nt": ((1,), (1,))}[kind]
    return lax.dot_general(a, b, (dims, ((), ())), preferred_element_type=FLOAT)


def dot3(a, b, kind="nn"):
    ah, al = split(a)
    bh, bl = split(b)
    return dot(ah, bh, kind) + (dot(ah, bl, kind) + dot(al, bh, kind))


def sin_cos(x):
    n = jnp.floor(x * (2.0 / math.pi) + 0.5)
    r = x - n * 1.5703125
    r = r - n * 4.837512969970703125e-4
    r = r - n * 7.549789948768648e-8
    z = r * r
    s = r + r * z * (-1.6666654611e-1 + z * (8.3321608736e-3 + z * -1.9515295891e-4))
    c = 1.0 - 0.5 * z + z * z * (4.166664568298827e-2 + z * (-1.388731625493765e-3 + z * 2.443315711809948e-5))
    q = n.astype(jnp.int32)
    odd = (q & 1) == 1
    sin = jnp.where(odd, c, s)
    cos = jnp.where(odd, s, c)
    sin = jnp.where((q & 2) == 2, -sin, sin)
    cos = jnp.where(((q + 1) & 2) == 2, -cos, cos)
    return sin, cos


def columns(parts):
    return jnp.concatenate(parts, axis=1)


def forward(signals, first, turn, middle):
    cos, sin = turn[0], turn[1]
    high, low = split(columns(signals))
    spec = dot(first[...], jnp.concatenate([high, low, high], axis=0))
    rows = []
    for i in range(len(signals)):
        re = spec[:ROWS, i * LANES : (i + 1) * LANES]
        im = spec[ROWS:, i * LANES : (i + 1) * LANES]
        rows.append(columns([re * cos + im * sin, im * cos - re * sin]))
    high, low = split(jnp.concatenate(rows, axis=0))
    return dot(high, middle[0]) + (dot(low, middle[0]) + dot(high, middle[1]))


def inverse(rows, last, turn, middle):
    cos, sin = turn[0], turn[1]
    high, low = split(jnp.concatenate(rows, axis=0))
    freq = dot(high, middle[2]) + (dot(low, middle[2]) + dot(high, middle[3]))
    cols = []
    for i in range(len(rows)):
        re = freq[i * ROWS : (i + 1) * ROWS, :LANES]
        im = freq[i * ROWS : (i + 1) * ROWS, LANES:]
        cols.append(jnp.concatenate([re * cos - im * sin, re * sin + im * cos], axis=0))
    high, low = split(columns(cols))
    return dot(last[...], jnp.concatenate([high, low, high], axis=0))


def times(a, b):
    ar, ai, br, bi = a[:, :LANES], a[:, LANES:], b[:, :LANES], b[:, LANES:]
    return columns([ar * br - ai * bi, ar * bi + ai * br])


def times_conj(a, b):
    ar, ai, br, bi = a[:, :LANES], a[:, LANES:], b[:, :LANES], b[:, LANES:]
    return columns([ar * br + ai * bi, ar * bi - ai * br])


def flipped(small):
    rows, cols = small.shape
    tall = jnp.concatenate([small, jnp.zeros((LANES - rows, cols), FLOAT)], axis=0)
    square = columns([tall, jnp.zeros((LANES, LANES - cols), FLOAT)]) if cols < LANES else tall
    return square.T


def remote(src, dst, send_sem, recv_sem, device):
    return pltpu.make_async_remote_copy(
        src_ref=src,
        dst_ref=dst,
        send_sem=send_sem,
        recv_sem=recv_sem,
        device_id=device,
        device_id_type=MESH,
    )


GROUP = 4
AREA = ROWS * OWN


def whole_kernel(
    rates_ref,
    proj_ref,
    taps_ref,
    cot_ref,
    emb_ref,
    w1_ref,
    w2_ref,
    wo_ref,
    first_ref,
    last_ref,
    turn_ref,
    middle_ref,
    mixed_ref,
    raw_ref,
    short_ref,
    out_ref,
    netf_ref,
    nets_ref,
    ext,
    ahead,
    feat,
    sends,
    got,
    backs,
    home,
    act1,
    cos1,
    act2,
    cos2,
    filt,
    fspec,
    pspec,
    small,
    small_dp,
    by_chan,
    outs,
    tiles,
    phase1,
    sum1,
    phase2,
    sum2,
    phase3,
    acc_out,
    acc_net,
    here,
    sent,
    came,
):
    me = lax.axis_index("seq")
    chan = lax.axis_index("chan")
    core = lax.axis_index("dp")
    z, xy = me // 16, lax.rem(me, 16)
    blocks = proj_ref.shape[3] // LANES
    barrier = pltpu.get_barrier_semaphore()

    load = pltpu.make_async_copy(proj_ref, ext.at[:, :, pl.ds(8, ROWS), :], here)
    load.start()

    def signal(**device):
        pl.semaphore_signal(barrier, inc=1, device_id=device, device_id_type=MESH)

    def greet(i, carry):
        signal(seq=lax.rem(me + i, ROWS))
        return carry

    lax.fori_loop(1, ROWS, greet, 0)
    for dz in range(4):
        signal(seq=lax.rem(z + dz, 4) * 16 + xy, dp=1 - core)
    for dc in range(1, 4):
        signal(chan=lax.rem(chan + dc, 4))
    load.wait()
    pl.semaphore_wait(barrier, ROWS - 1 + 7)

    rim = remote(
        ext.at[:, :, pl.ds(ROWS, 8), :],
        ext.at[:, :, pl.ds(0, 8), :],
        sent.at[0],
        came.at[0],
        {"seq": lax.rem(me + 1, ROWS)},
    )
    rim.start()
    rim.wait()

    @pl.when(me == 0)
    def _():
        ext[:, :, :8, :] = jnp.zeros((3, 2, 8, ext.shape[3]), FLOAT)

    def lanes(b):
        return pl.ds(pl.multiple_of(b * LANES, LANES), LANES)

    def tapped(i, w, cols):
        total = taps_ref[i, 0:1, cols] * ext[i, w, 8:, cols]
        for j in range(1, RIM + 1):
            total = total + taps_ref[i, j : j + 1, cols] * ext[i, w, 8 - j : 8 - j + ROWS, cols]
        feat[i, w, :, cols] = total
        return total

    def to_peers(source, target, signal_at, sem):
        base = signal_at * AREA
        mine = pl.ds(pl.multiple_of(base + me * OWN, OWN), OWN)
        target[mine, :] = source[mine, :]

        def send(i, carry):
            px = lax.rem(lax.rem(me // 4, 4) + lax.rem(i // 4, 4), 4)
            py = lax.rem(lax.rem(me, 4) + i // 16, 4)
            peer = lax.rem(z + lax.rem(i, 4), 4) * 16 + px * 4 + py
            block = pl.ds(pl.multiple_of(base + peer * OWN, OWN), OWN)
            remote(source.at[block], target.at[mine], sent.at[sem], came.at[sem], {"seq": peer}).start()
            return carry

        lax.fori_loop(1, ROWS, send, 0)

    def peers_done(ref, sem):
        part = ref.at[pl.ds(0, AREA - OWN)]
        return remote(part, part, sent.at[sem], came.at[sem], {"seq": me})

    def products(b, carry):
        cols = lanes(b)
        parts = [tapped(1, w, cols) * tapped(2, w, cols) for w in range(2)]
        rows = pl.ds(pl.multiple_of(b * LANES, LANES), LANES)
        sends[rows, :] = jnp.concatenate(parts, axis=0).T
        return carry

    lax.fori_loop(0, blocks, products, 0)
    to_peers(sends, got, 0, 1)

    def gradients(b, carry):
        cols = lanes(b)
        parts = [tapped(0, w, cols) * cot_ref[w, :, cols] for w in range(2)]
        rows = pl.ds(pl.multiple_of(AREA + b * LANES, LANES), LANES)
        sends[rows, :] = jnp.concatenate(parts, axis=0).T
        return carry

    lax.fori_loop(0, blocks, gradients, 0)
    to_peers(sends, got, 1, 2)

    turned = pltpu.roll(
        wo_ref[:, lanes(me // 8)], lax.rem(LANES - lax.rem(me, 8) * OWN, LANES), 1
    )
    wo_own = turned[:, :OWN]
    wo_t = flipped(turned)[:OWN, :ROWS]
    w1_t = flipped(w1_ref[...])[:ROWS, : w1_ref.shape[0]]
    w2_t = flipped(w2_ref[...])[:ROWS, :ROWS]
    lane = lax.broadcasted_iota(jnp.int32, (OWN, LANES), 1)
    low_half = lane < ROWS

    def net(step, carry):
        cols = pl.ds(pl.multiple_of(step * STEP, STEP), STEP)
        s1, c1 = sin_cos(dot3(w1_t, emb_ref[:, cols]))
        act1[:, cols] = s1
        cos1[:, cols] = c1
        s2, c2 = sin_cos(dot3(w2_t, s1))
        act2[:, cols] = s2
        cos2[:, cols] = c2
        raw = dot3(wo_t, s2)
        for pair in range(STEP // LANES):
            both = raw[:, pair * LANES : (pair + 1) * LANES]
            other = pltpu.roll(both, ROWS, 1)
            base = pl.multiple_of((step * (STEP // ROWS) + 2 * pair) * OWN, OWN)
            filt[pl.ds(base, OWN), :] = jnp.where(low_half, both, other)
            filt[pl.ds(base + OWN, OWN), :] = jnp.where(low_half, other, both)
        return carry

    lax.fori_loop(0, SEQ // STEP, net, 0)

    place = lax.broadcasted_iota(jnp.int32, (ROWS, LANES), 0) * ROWS + (
        lax.broadcasted_iota(jnp.int32, (ROWS, LANES), 1) & (ROWS - 1)
    )
    place = place.astype(FLOAT)

    def envelope(ch):
        rate = rates_ref[me * OWN + ch]
        return jnp.exp(place * -rate) * jnp.sqrt(jnp.full((1, LANES), 2.0 * rate + 1.0 / SEQ, FLOAT))

    def strided(ref, base, ch):
        return ref[pl.ds(base + ch, ROWS, stride=OWN), :]

    def group_rows(step):
        return pl.ds(pl.multiple_of(step * GROUP * ROWS, GROUP * ROWS), GROUP * ROWS)

    def cut(value):
        return [value[i * ROWS : (i + 1) * ROWS] for i in range(GROUP)]

    def filters(step, carry):
        chans = [step * GROUP + i for i in range(GROUP)]
        signals = [strided(filt, 0, ch) * envelope(ch) for ch in chans]
        fspec[group_rows(step), :] = forward(signals, first_ref, turn_ref, middle_ref)
        return carry

    lax.fori_loop(0, OWN // GROUP, filters, 0)

    def put(value, base, step):
        for i in range(GROUP):
            backs[pl.ds(base + step * GROUP + i, ROWS, stride=OWN), :] = value[
                :, i * LANES : (i + 1) * LANES
            ]

    peers_done(got, 1).wait_recv()

    def convolve(step, carry):
        signals = [strided(got, 0, step * GROUP + i) for i in range(GROUP)]
        spec = forward(signals, first_ref, turn_ref, middle_ref)
        pspec[group_rows(step), :] = spec
        rows = cut(times(spec, fspec[group_rows(step), :]))
        put(inverse(rows, last_ref, turn_ref, middle_ref), 0, step)
        return carry

    lax.fori_loop(0, OWN // GROUP, convolve, 0)
    to_peers(backs, home, 0, 3)
    peers_done(got, 2).wait_recv()

    def correlate(step, carry):
        signals = [strided(got, AREA, step * GROUP + i) for i in range(GROUP)]
        spec = forward(signals, first_ref, turn_ref, middle_ref)
        rows = cut(times_conj(fspec[group_rows(step), :], spec))
        put(inverse(rows, last_ref, turn_ref, middle_ref), AREA, step)
        pair = times_conj(pspec[group_rows(step), :], spec)
        re, im = pair[:, :LANES], pair[:, LANES:]
        pspec[group_rows(step), :] = columns(
            [re + pltpu.roll(re, ROWS, 1), im + pltpu.roll(im, ROWS, 1)]
        )
        return carry

    lax.fori_loop(0, OWN // GROUP, correlate, 0)
    to_peers(backs, home, 1, 4)

    def filter_back(step, carry):
        rows = cut(pspec[group_rows(step), :])
        value = inverse(rows, last_ref, turn_ref, middle_ref)
        for i in range(GROUP):
            ch = step * GROUP + i
            filt[pl.ds(ch, ROWS, stride=OWN), :] = value[:, i * LANES : (i + 1) * LANES] * envelope(ch)
        return carry

    lax.fori_loop(0, OWN // GROUP, filter_back, 0)
    acc_out[...] = jnp.zeros_like(acc_out)
    acc_net[...] = jnp.zeros_like(acc_net)

    def net_back(step, carry):
        cols = pl.ds(pl.multiple_of(step * STEP, STEP), STEP)
        parts = []
        for pair in range(STEP // LANES):
            base = pl.multiple_of((step * (STEP // ROWS) + 2 * pair) * OWN, OWN)
            parts.append(jnp.where(low_half, filt[pl.ds(base, OWN), :], filt[pl.ds(base + OWN, OWN), :]))
        kgrad = columns(parts)
        acc_out[...] += dot3(kgrad, act2[:, cols], "nt")
        pre2 = dot3(wo_own, kgrad) * cos2[:, cols]
        acc_net[32:, :] += dot3(act1[:, cols], pre2, "nt")
        pre1 = dot3(w2_ref[...], pre2) * cos1[:, cols]
        acc_net[:32, :] += dot3(emb_ref[:, cols], pre1, "nt")
        return carry

    lax.fori_loop(0, SEQ // STEP, net_back, 0)
    small[:48, :] = columns([acc_net[:48, :], acc_net[48:, :]])
    small[48:, :] = columns([acc_out[:8, :], acc_out[8:, :]])
    swap = remote(small, small_dp, sent.at[5], came.at[5], {"dp": 1 - core})
    swap.start()
    swap.wait()
    total = small[...] + small_dp[...]
    by_chan[chan] = total[:48]
    outs[z, xy] = total[48:]
    for d in range(1, 4):
        remote(by_chan.at[chan], by_chan.at[chan], sent.at[6], came.at[6], {"chan": lax.rem(chan + d, 4)}).start()
        remote(outs.at[z, xy], outs.at[z, xy], sent.at[7], came.at[7], {"seq": lax.rem(z + d, 4) * 16 + xy}).start()
    chans_done = remote(by_chan.at[pl.ds(0, 3)], by_chan.at[pl.ds(0, 3)], sent.at[6], came.at[6], {"seq": me})
    zs_done = remote(outs.at[pl.ds(0, 3), 0], outs.at[pl.ds(0, 3), 0], sent.at[7], came.at[7], {"seq": me})
    zs_done.wait()

    def around(i):
        return lax.rem(xy // 4 + i // 4, 4) * 4 + lax.rem(lax.rem(xy, 4) + lax.rem(i, 4), 4)

    def spread_outs(i, carry):
        column = outs.at[:, xy]
        remote(column, column, sent.at[8], came.at[8], {"seq": z * 16 + around(i)}).start()
        return carry

    lax.fori_loop(1, 16, spread_outs, 0)
    chans_done.wait()
    net_sum = (by_chan[0] + by_chan[1]) + (by_chan[2] + by_chan[3])
    for i in range(6):
        tiles[24 + i] = net_sum[i * 8 : (i + 1) * 8]
    tiles[30] = jnp.zeros((8, LANES), FLOAT)
    tiles[31] = jnp.zeros((8, LANES), FLOAT)

    peers_done(home, 3).wait_recv()

    def mix(b, carry):
        cols = lanes(b)
        conv = home[pl.ds(pl.multiple_of(b * LANES, LANES), LANES), :].T
        for w in range(2):
            part = conv[w * ROWS : (w + 1) * ROWS]
            mixed_ref[w, :, cols] = feat[0, w, :, cols] * part
            ahead[0, w, :ROWS, cols] = cot_ref[w, :, cols] * part
        return carry

    lax.fori_loop(0, blocks, mix, 0)
    peers_done(home, 4).wait_recv()

    def unmix(b, carry):
        cols = lanes(b)
        back = home[pl.ds(pl.multiple_of(AREA + b * LANES, LANES), LANES), :].T
        for w in range(2):
            part = back[w * ROWS : (w + 1) * ROWS]
            ahead[1, w, :ROWS, cols] = part * feat[2, w, :, cols]
            ahead[2, w, :ROWS, cols] = part * feat[1, w, :, cols]
        return carry

    lax.fori_loop(0, blocks, unmix, 0)
    after = remote(
        ahead.at[:, :, pl.ds(0, 8), :],
        ahead.at[:, :, pl.ds(ROWS, 8), :],
        sent.at[9],
        came.at[9],
        {"seq": lax.rem(me + ROWS - 1, ROWS)},
    )
    after.start()

    def tap_sums(b, carry):
        cols = lanes(b)
        for i in range(3):
            sums = []
            for j in range(RIM + 1):
                both = ahead[i, 0, :ROWS, cols] * ext[i, 0, 8 - j : 8 - j + ROWS, cols]
                both = both + ahead[i, 1, :ROWS, cols] * ext[i, 1, 8 - j : 8 - j + ROWS, cols]
                sums.append(jnp.sum(both, axis=0, keepdims=True))
            sums.append(jnp.zeros((1, LANES), FLOAT))
            tiles[i * 8 + b] = jnp.concatenate(sums, axis=0)
        return carry

    lax.fori_loop(0, blocks, tap_sums, 0)

    phase1[xy] = tiles[pl.ds(2 * xy, 2)]

    def scatter(i, carry):
        q = around(i)
        remote(tiles.at[pl.ds(2 * q, 2)], phase1.at[xy], sent.at[10], came.at[10], {"seq": z * 16 + q}).start()
        return carry

    lax.fori_loop(1, 16, scatter, 0)
    after.wait()

    @pl.when(me == ROWS - 1)
    def _():
        ahead[:, :, ROWS:, :] = jnp.zeros((3, 2, 8, ahead.shape[3]), FLOAT)

    def raws(b, carry):
        cols = lanes(b)
        for i in range(3):
            for w in range(2):
                total = taps_ref[i, 0:1, cols] * ahead[i, w, :ROWS, cols]
                for j in range(1, RIM + 1):
                    total = total + taps_ref[i, j : j + 1, cols] * ahead[i, w, j : j + ROWS, cols]
                raw_ref[i, w, :, cols] = total
        return carry

    lax.fori_loop(0, blocks, raws, 0)
    first15 = phase1.at[pl.ds(0, 15)]
    remote(first15, first15, sent.at[10], came.at[10], {"seq": me}).wait()
    sum1[...] = jnp.sum(phase1[...], axis=0)
    phase2[z * 2 + core] = sum1[...]
    for dz in range(4):
        for dc in range(2):
            if dz or dc:
                to = lax.rem(z + dz, 4) * 16 + xy
                remote(sum1, phase2.at[z * 2 + core], sent.at[11], came.at[11], {"seq": to, "dp": lax.rem(core + dc, 2)}).start()
    first7 = phase2.at[pl.ds(0, 7)]
    remote(first7, first7, sent.at[11], came.at[11], {"seq": me}).wait()
    sum2[...] = jnp.sum(phase2[...], axis=0)
    phase3[xy] = sum2[...]

    def gather(i, carry):
        remote(sum2, phase3.at[xy], sent.at[12], came.at[12], {"seq": z * 16 + around(i)}).start()
        return carry

    lax.fori_loop(1, 16, gather, 0)

    outs_part = outs.at[:, pl.ds(0, 15)]
    remote(outs_part, outs_part, sent.at[8], came.at[8], {"seq": me}).wait()
    windows = 4
    tail = 1.0 / math.sqrt(windows * SEQ)
    scale = 2.0 / math.sqrt(windows * SEQ * blocks * LANES * 4)
    for b in range(blocks):
        rows = []
        for s in range(8 * b, 8 * b + 8):
            tile = outs[s // 16, s % 16]
            rows += [tile, pltpu.roll(tile, ROWS, 1)]
        square = jnp.concatenate(rows, axis=0).T
        out_ref[:, b * LANES : (b + 1) * LANES] = square[:ROWS] * tail

    last15 = phase3.at[pl.ds(0, 15)]
    remote(last15, last15, sent.at[12], came.at[12], {"seq": me}).wait()
    for i in range(3):
        for b in range(blocks):
            t = i * 8 + b
            short_ref[i, :, b * LANES : (b + 1) * LANES] = phase3[t // 2, t % 2][: RIM + 1] * tail
    net_sum = jnp.concatenate([phase3[t // 2, t % 2] for t in range(24, 30)], axis=0) * scale
    netf_ref[...] = net_sum[:32, :ROWS]
    nets_ref[:16, :] = net_sum[32:, :ROWS]
    nets_ref[16:, :] = net_sum[:, ROWS:]
    for sem in (1, 2):
        peers_done(sends, sem).wait_send()
    for sem in (3, 4):
        peers_done(backs, sem).wait_send()


def shards(projected, short_weight, decay_rates, w1, w2, out_weight, cotangent):
    first_stack, last_stack, turn, middle, embedded = tables()
    vmem = pl.BlockSpec(memory_space=pltpu.VMEM)
    group = projected.shape[3]
    hidden = w2.shape[0]

    def buffer(*shape):
        return pltpu.VMEM(shape, FLOAT)

    def like(value):
        return jax.ShapeDtypeStruct(value.shape, FLOAT)

    rows = projected.shape[2] + 8
    return pl.pallas_call(
        whole_kernel,
        out_shape=(
            like(cotangent),
            like(projected),
            like(short_weight),
            like(out_weight),
            like(w1),
            like(w2),
        ),
        in_specs=[pl.BlockSpec(memory_space=pltpu.SMEM), pl.BlockSpec(memory_space=pl.ANY)] + [vmem] * 10,
        out_specs=(vmem,) * 6,
        scratch_shapes=[
            buffer(3, 2, rows, group),
            buffer(3, 2, rows, group),
            buffer(3, 2, ROWS, group),
            buffer(2 * AREA, LANES),
            buffer(2 * AREA, LANES),
            buffer(2 * AREA, LANES),
            buffer(2 * AREA, LANES),
            buffer(hidden, SEQ),
            buffer(hidden, SEQ),
            buffer(hidden, SEQ),
            buffer(hidden, SEQ),
            buffer(AREA, LANES),
            buffer(AREA, 2 * LANES),
            buffer(AREA, 2 * LANES),
            buffer(56, LANES),
            buffer(56, LANES),
            buffer(4, 48, LANES),
            buffer(4, 16, 8, LANES),
            buffer(32, 8, LANES),
            buffer(16, 2, 8, LANES),
            buffer(2, 8, LANES),
            buffer(8, 2, 8, LANES),
            buffer(2, 8, LANES),
            buffer(16, 2, 8, LANES),
            buffer(OWN, hidden),
            buffer(96, hidden),
            pltpu.SemaphoreType.DMA,
            pltpu.SemaphoreType.DMA((13,)),
            pltpu.SemaphoreType.DMA((13,)),
        ],
        compiler_params=pltpu.CompilerParams(
            collective_id=1, has_side_effects=True, vmem_limit_bytes=52 << 20
        ),
        name="whole",
    )(
        decay_rates,
        projected,
        short_weight,
        cotangent,
        jnp.asarray(embedded),
        w1,
        w2,
        out_weight,
        jnp.asarray(first_stack),
        jnp.asarray(last_stack),
        jnp.asarray(turn),
        jnp.asarray(middle),
    )


def solution(mesh):
    return jax.shard_map(
        shards,
        mesh=mesh,
        in_specs=(
            P(None, "dp", "seq", "chan"),
            P(None, None, "chan"),
            P("chan"),
            P(),
            P(),
            P(None, "chan"),
            P("dp", "seq", "chan"),
        ),
        out_specs=(
            P("dp", "seq", "chan"),
            P(None, "dp", "seq", "chan"),
            P(None, None, "chan"),
            P(None, "chan"),
            P(),
            P(),
        ),
        check_vma=False,
    )
```

time: 291 us -> 190 us (0.65)
  Pallas kernels: 237 us -> 174 us
  starting transfers between devices: 27.6 us -> 0 us
  other arithmetic: 5.6 us -> 0 us
  waiting for transfers between devices: 4.53 us -> 0 us
    pallas_call x8 -> x1, Pallas kernels: 237 us -> 174 us  [shards(): pl.pallas_call(whole_kernel, out_shape=(like(cotangent), like(projected),...]
    ppermute x6 -> x0, starting transfers between devices: 27.6 us -> none  [the longest x4 22.3 us: swapped(): return lax.ppermute(value, axis, [(i, i ^ bit) for i in range(count)])]
    unnamed x28 -> x22, local copies, waits for them, and re-layouts: 6.24 us -> 12.6 us
    ppermute x6 -> x0, waiting for transfers between devices: 4.53 us -> none  [the longest x4 3.41 us: swapped(): return lax.ppermute(value, axis, [(i, i ^ bit) for i in range(count)])]
    slice x7 -> x0, local copies, waits for them, and re-layouts: 2.99 us -> none  [the longest x1 0.98 us: shards(): projected[:, :, ROWS - 8:, :]]
  transfers between devices with their start and end apart: 6 -> 0, of which waited for: 3 -> 0; matrix products, arithmetic and copies ran while one was open for 1% -> 0% of each run, Pallas kernels for 2% -> 0%
where the time goes in v2:
time: 190 us; the launch traced here: 187 us
  Pallas kernels  174 us (92%)
  local copies, waits for them, and re-layouts  12.6 us (7%)
    pallas_call x1, Pallas kernels, shards(): pl.pallas_call(whole_kernel, out_shape=(like(cotangent), like(projected),...  174 us
    unnamed x22, local copies, waits for them, and re-layouts  12.6 us

profile of v2, /device:TPU:1, one launch (start us, length us, event | category | flops | bytes accessed | tf_op | source)
XLA Modules:
  0.0 187.5 jit_solution(8021917958082238720)
XLA Ops:
  0.6 0.0 copy-start
  0.6 0.9 copy-done
  1.6 0.0 copy-start.1
  1.6 0.9 copy-done.1
  2.5 0.0 copy-start.2
  2.5 0.8 copy-done.2
  3.3 0.0 copy-start.3
  3.3 0.8 copy-done.3
  4.2 0.0 copy-start.4
  4.2 0.8 copy-done.4
  5.0 0.0 copy-start.5
  5.0 0.8 copy-done.5
  5.7 0.0 copy-start.6
  5.7 0.7 copy-done.6
  6.4 0.0 copy-start.7
  6.4 0.7 copy-done.7
  7.1 174.2 %whole.1 = (f32[2,64,1024]{2,1,0:T(8,128)S(1)}, f32[3,2,64,1024]{3,2,1,0:T(8,128)}, f32[3,7,1024]{2,1,0:T(8,128)S(1)}, f32[64,1024]{1,0:T(8,128)S(1)}, f32[32,64]{1,0:T(8,128)S(1)}, /*index=5*/f32[64,64]{1,0:T(8,128)S(1)}) custom-call(f32[1024]{0:T(1024)S(1)} %copy-done.7, f32[3,2,64,1024]{3,2,1,0:T(8,128)} %proj_ref.1, f32[3,7,1024]{2,1,0:T(8,128)S(1)} %copy-done.1, ...), custom_call_target="tpu_custom_call" | custom-call | tf_op jit(solution)/shard_map/whole/pallas_call | solution.py:570
  181.4 0.8 copy.24
  182.2 2.7 %copy.25 = f32[3,2,64,1024]{3,2,1,0:T(8,128)} copy(f32[3,2,64,1024]{3,2,1,0:T(8,128)} %get-tuple-element.13) | data formatting | bytes 3145728
  184.9 0.6 copy.26
  185.5 0.7 copy.27
  186.2 0.6 copy.28
  186.8 0.6 copy.29
Async XLA Ops:
  0.6 1.0 copy-start
  1.6 0.9 copy-start.1
  2.5 0.8 copy-start.2
  3.3 0.8 copy-start.3
  4.2 0.8 copy-start.4
  5.0 0.8 copy-start.5
  5.7 0.7 copy-start.6
  6.4 0.7 copy-start.7

commit v3 on v2

--- a/solution.py
+++ b/solution.py
@@ -50,7 +50,7 @@
     factors = 1 + (SEQ // 2 - 2) * orders * orders // max((half - 1) ** 2, 1)
     angle = 2 * np.pi * (factors[:, None] * np.arange(SEQ)[None, :] % SEQ) / SEQ
     embedded = np.concatenate([np.cos(angle), np.sin(angle)], axis=0).astype(np.float32)
-    return first_stack, last_stack, turn, middle, embedded
+    return (*(t.astype(np.float32) for t in (first_stack, last_stack)), turn, middle.astype(np.float32), embedded)
 
 
 def split(value):
@@ -150,23 +150,38 @@
 
 def whole_kernel(
     rates_ref,
-    proj_ref,
+    proj_hbm,
+    taps_hbm,
+    cot_hbm,
+    emb_hbm,
+    w1_hbm,
+    w2_hbm,
+    wo_hbm,
+    first_hbm,
+    last_hbm,
+    turn_hbm,
+    middle_hbm,
+    mixed_hbm,
+    raw_hbm,
+    short_ref,
+    out_ref,
+    netf_ref,
+    nets_ref,
     taps_ref,
     cot_ref,
     emb_ref,
     w1_ref,
     w2_ref,
     wo_ref,
+    first_wide,
+    last_wide,
+    turn_ref,
+    middle_wide,
     first_ref,
     last_ref,
-    turn_ref,
     middle_ref,
     mixed_ref,
     raw_ref,
-    short_ref,
-    out_ref,
-    netf_ref,
-    nets_ref,
     ext,
     ahead,
     feat,
@@ -181,8 +196,8 @@
     filt,
     fspec,
     pspec,
-    small,
-    small_dp,
+    out_mine,
+    out_dp,
     by_chan,
     outs,
     tiles,
@@ -193,7 +208,15 @@
     phase3,
     acc_out,
     acc_net,
-    here,
+    edge_kv,
+    rim_kv,
+    relay,
+    after_kv_rows,
+    edge_q,
+    rim_q,
+    after_q_rows,
+    loads,
+    saves,
     sent,
     came,
 ):
@@ -201,50 +224,62 @@
     chan = lax.axis_index("chan")
     core = lax.axis_index("dp")
     z, xy = me // 16, lax.rem(me, 16)
-    blocks = proj_ref.shape[3] // LANES
+    x, y = xy // 4, lax.rem(xy, 4)
+    following, previous = lax.rem(me + 1, ROWS), lax.rem(me + ROWS - 1, ROWS)
+    blocks = feat.shape[3] // LANES
     barrier = pltpu.get_barrier_semaphore()
 
-    load = pltpu.make_async_copy(proj_ref, ext.at[:, :, pl.ds(8, ROWS), :], here)
-    load.start()
-
-    def signal(**device):
-        pl.semaphore_signal(barrier, inc=1, device_id=device, device_id_type=MESH)
-
-    def greet(i, carry):
-        signal(seq=lax.rem(me + i, ROWS))
-        return carry
-
-    lax.fori_loop(1, ROWS, greet, 0)
-    for dz in range(4):
-        signal(seq=lax.rem(z + dz, 4) * 16 + xy, dp=1 - core)
-    for dc in range(1, 4):
-        signal(chan=lax.rem(chan + dc, 4))
-    load.wait()
-    pl.semaphore_wait(barrier, ROWS - 1 + 7)
-
-    rim = remote(
-        ext.at[:, :, pl.ds(ROWS, 8), :],
-        ext.at[:, :, pl.ds(0, 8), :],
-        sent.at[0],
-        came.at[0],
-        {"seq": lax.rem(me + 1, ROWS)},
-    )
-    rim.start()
-    rim.wait()
-
-    @pl.when(me == 0)
-    def _():
-        ext[:, :, :8, :] = jnp.zeros((3, 2, 8, ext.shape[3]), FLOAT)
-
+    def signal(sem, **device):
+        pl.semaphore_signal(sem, inc=1, device_id=device, device_id_type=MESH)
+
+    for dz in (2, 1, 3, 0):
+        plane = lax.rem(z + dz, 4) * 16
+
+        def greet(i, carry):
+            signal(barrier, seq=plane + lax.rem(xy + i, 16))
+            return carry
+
+        lax.fori_loop(0 if dz else 1, 16, greet, 0)
+        signal(barrier, seq=plane + xy, dp=1 - core)
+    for d in range(1, 4):
+        signal(barrier, chan=lax.rem(chan + d, 4))
+
+    pairs = [
+        (proj_hbm, ext.at[:, :, pl.ds(8, ROWS), :]),
+        (taps_hbm, taps_ref),
+        (cot_hbm, cot_ref),
+        (emb_hbm, emb_ref),
+        (w1_hbm, w1_ref),
+        (w2_hbm, w2_ref),
+        (wo_hbm, wo_ref),
+        (first_hbm, first_wide),
+        (last_hbm, last_wide),
+        (turn_hbm, turn_ref),
+        (middle_hbm, middle_wide),
+    ]
+    copies = [pltpu.make_async_copy(src, dst, loads.at[i]) for i, (src, dst) in enumerate(pairs)]
+    for copy in copies:
+        copy.start()
+    copies[0].wait()
+    copies[1].wait()
     def lanes(b):
         return pl.ds(pl.multiple_of(b * LANES, LANES), LANES)
 
-    def tapped(i, w, cols):
-        total = taps_ref[i, 0:1, cols] * ext[i, w, 8:, cols]
+    def tapped(i, w, cols, start, count):
+        total = taps_ref[i, 0:1, cols] * ext[i, w, 8 + start : 8 + start + count, cols]
         for j in range(1, RIM + 1):
-            total = total + taps_ref[i, j : j + 1, cols] * ext[i, w, 8 - j : 8 - j + ROWS, cols]
-        feat[i, w, :, cols] = total
-        return total
+            rows = slice(8 + start - j, 8 + start - j + count)
+            total = total + taps_ref[i, j : j + 1, cols] * ext[i, w, rows, cols]
+        feat[i, w, start : start + count, cols] = total
+
+    def later_rows(group):
+        def body(b, carry):
+            for i in group:
+                for w in range(2):
+                    tapped(i, w, lanes(b), 8, ROWS - 8)
+            return carry
+
+        lax.fori_loop(0, blocks, body, 0)
 
     def to_peers(source, target, signal_at, sem):
         base = signal_at * AREA
@@ -252,8 +287,7 @@
         target[mine, :] = source[mine, :]
 
         def send(i, carry):
-            px = lax.rem(lax.rem(me // 4, 4) + lax.rem(i // 4, 4), 4)
-            py = lax.rem(lax.rem(me, 4) + i // 16, 4)
+            px, py = lax.rem(x + lax.rem(i // 4, 4), 4), lax.rem(y + i // 16, 4)
             peer = lax.rem(z + lax.rem(i, 4), 4) * 16 + px * 4 + py
             block = pl.ds(pl.multiple_of(base + peer * OWN, OWN), OWN)
             remote(source.at[block], target.at[mine], sent.at[sem], came.at[sem], {"seq": peer}).start()
@@ -265,25 +299,96 @@
         part = ref.at[pl.ds(0, AREA - OWN)]
         return remote(part, part, sent.at[sem], came.at[sem], {"seq": me})
 
+    def pack(buffer, features, row):
+        for n, (i, w) in enumerate((i, w) for i in features for w in range(2)):
+            yield n * RIM, buffer.at[i, w, pl.ds(row, RIM), :]
+
+    def packed(target, buffer, features, row):
+        for at, part in pack(buffer, features, row):
+            target[at : at + RIM, :] = part[...]
+
+    def unpacked(source, buffer, features, row):
+        for at, part in pack(buffer, features, row):
+            part[...] = source[at : at + RIM, :]
+
+    def no_rows(buffer, features, row, where):
+        @pl.when(me == where)
+        def _():
+            for i in features:
+                buffer[i, :, row : row + 8, :] = jnp.zeros((2, 8, buffer.shape[3]), FLOAT)
+
+    keys = (1, 2)
+    edge_q[8:, :] = jnp.zeros((8, edge_q.shape[1]), FLOAT)
+    packed(edge_kv, ext, keys, ROWS + 8 - RIM)
+    packed(edge_q, ext, (0,), ROWS + 8 - RIM)
+    later_rows(keys)
+    later_rows((0,))
+    pl.semaphore_wait(barrier, ROWS - 1 + 7)
+
+    quarter = edge_kv.shape[1] // 4
+    ahead_plane = lax.rem(z + 1, 4) * 16
+
+    def piece(ref, c):
+        return ref.at[:, c * quarter : (c + 1) * quarter]
+
+    @pl.when(xy != 15)
+    def _():
+        remote(edge_kv, rim_kv, sent.at[0], came.at[0], {"seq": following}).start()
+
+    @pl.when(xy == 15)
+    def _():
+        for c, via in enumerate((3, 12, 0)):
+            to = {"seq": z * 16 + via}
+            remote(piece(edge_kv, c), piece(relay, c), sent.at[0], came.at[16], to).start()
+        remote(piece(edge_kv, 3), piece(rim_kv, 3), sent.at[0], came.at[0], {"seq": following}).start()
+
+    for c, via in enumerate((3, 12, 0)):
+
+        @pl.when(xy == via)
+        def _(c=c):
+            part = piece(relay, c)
+            remote(part, part, sent.at[16], came.at[16], {"seq": me}).wait_recv()
+            on = remote(part, piece(rim_kv, c), sent.at[16], came.at[0], {"seq": ahead_plane})
+            on.start()
+            on.wait_send()
+
+    remote(rim_kv, rim_kv, sent.at[0], came.at[0], {"seq": me}).wait()
+    to_q = remote(edge_q, rim_q, sent.at[13], came.at[13], {"seq": following})
+    to_q.start()
+    unpacked(rim_kv, ext, keys, 8 - RIM)
+    no_rows(ext, keys, 0, 0)
+
     def products(b, carry):
         cols = lanes(b)
-        parts = [tapped(1, w, cols) * tapped(2, w, cols) for w in range(2)]
-        rows = pl.ds(pl.multiple_of(b * LANES, LANES), LANES)
-        sends[rows, :] = jnp.concatenate(parts, axis=0).T
+        for i in (1, 2):
+            for w in range(2):
+                tapped(i, w, cols, 0, 8)
+        parts = [feat[1, w, :, cols] * feat[2, w, :, cols] for w in range(2)]
+        sends[lanes(b), :] = jnp.concatenate(parts, axis=0).T
         return carry
 
     lax.fori_loop(0, blocks, products, 0)
     to_peers(sends, got, 0, 1)
+    to_q.wait()
+    unpacked(rim_q, ext, (0,), 8 - RIM)
+    no_rows(ext, (0,), 0, 0)
+    copies[2].wait()
 
     def gradients(b, carry):
         cols = lanes(b)
-        parts = [tapped(0, w, cols) * cot_ref[w, :, cols] for w in range(2)]
+        for w in range(2):
+            tapped(0, w, cols, 0, 8)
+        parts = [feat[0, w, :, cols] * cot_ref[w, :, cols] for w in range(2)]
         rows = pl.ds(pl.multiple_of(AREA + b * LANES, LANES), LANES)
         sends[rows, :] = jnp.concatenate(parts, axis=0).T
         return carry
 
     lax.fori_loop(0, blocks, gradients, 0)
-    to_peers(sends, got, 1, 2)
+    for copy in copies[3:]:
+        copy.wait()
+    first_ref[...] = first_wide[...].astype(HALF)
+    last_ref[...] = last_wide[...].astype(HALF)
+    middle_ref[...] = middle_wide[...].astype(HALF)
 
     turned = pltpu.roll(
         wo_ref[:, lanes(me // 8)], lax.rem(LANES - lax.rem(me, 8) * OWN, LANES), 1
@@ -339,6 +444,7 @@
         return carry
 
     lax.fori_loop(0, OWN // GROUP, filters, 0)
+    to_peers(sends, got, 1, 2)
 
     def put(value, base, step):
         for i in range(GROUP):
@@ -402,27 +508,28 @@
         return carry
 
     lax.fori_loop(0, SEQ // STEP, net_back, 0)
-    small[:48, :] = columns([acc_net[:48, :], acc_net[48:, :]])
-    small[48:, :] = columns([acc_out[:8, :], acc_out[8:, :]])
-    swap = remote(small, small_dp, sent.at[5], came.at[5], {"dp": 1 - core})
+    out_mine[...] = columns([acc_out[:8, :], acc_out[8:, :]])
+    by_chan[chan] = columns([acc_net[:48, :], acc_net[48:, :]])
+    swap = remote(out_mine, out_dp, sent.at[5], came.at[5], {"dp": 1 - core})
     swap.start()
+    for d in range(1, 4):
+        part = by_chan.at[chan]
+        remote(part, part, sent.at[6], came.at[6], {"chan": lax.rem(chan + d, 4)}).start()
     swap.wait()
-    total = small[...] + small_dp[...]
-    by_chan[chan] = total[:48]
-    outs[z, xy] = total[48:]
+    outs[z, xy] = out_mine[...] + out_dp[...]
     for d in range(1, 4):
-        remote(by_chan.at[chan], by_chan.at[chan], sent.at[6], came.at[6], {"chan": lax.rem(chan + d, 4)}).start()
-        remote(outs.at[z, xy], outs.at[z, xy], sent.at[7], came.at[7], {"seq": lax.rem(z + d, 4) * 16 + xy}).start()
+        part = outs.at[z, xy]
+        remote(part, part, sent.at[7], came.at[7], {"seq": lax.rem(z + d, 4) * 16 + xy}).start()
     chans_done = remote(by_chan.at[pl.ds(0, 3)], by_chan.at[pl.ds(0, 3)], sent.at[6], came.at[6], {"seq": me})
     zs_done = remote(outs.at[pl.ds(0, 3), 0], outs.at[pl.ds(0, 3), 0], sent.at[7], came.at[7], {"seq": me})
     zs_done.wait()
 
     def around(i):
-        return lax.rem(xy // 4 + i // 4, 4) * 4 + lax.rem(lax.rem(xy, 4) + lax.rem(i, 4), 4)
+        return z * 16 + lax.rem(x + i // 4, 4) * 4 + lax.rem(y + lax.rem(i, 4), 4)
 
     def spread_outs(i, carry):
         column = outs.at[:, xy]
-        remote(column, column, sent.at[8], came.at[8], {"seq": z * 16 + around(i)}).start()
+        remote(column, column, sent.at[8], came.at[8], {"seq": around(i)}).start()
         return carry
 
     lax.fori_loop(1, 16, spread_outs, 0)
@@ -433,11 +540,76 @@
     tiles[30] = jnp.zeros((8, LANES), FLOAT)
     tiles[31] = jnp.zeros((8, LANES), FLOAT)
 
+    def scatter():
+        phase1[xy] = tiles[pl.ds(2 * xy, 2)]
+
+        def send(i, carry):
+            q = around(i)
+            part = tiles.at[pl.ds(2 * (q - z * 16), 2)]
+            remote(part, phase1.at[xy], sent.at[10], came.at[10], {"seq": q}).start()
+            return carry
+
+        lax.fori_loop(1, 16, send, 0)
+
+    def exchange():
+        first15 = phase1.at[pl.ds(0, 15)]
+        remote(first15, first15, sent.at[10], came.at[10], {"seq": me}).wait()
+        sum1[...] = jnp.sum(phase1[...], axis=0)
+        mine = phase2.at[z * 2 + core]
+        phase2[z * 2 + core] = sum1[...]
+        for dz in (2, 1, 3, 0):
+            for dc in (0, 1):
+                if dz or dc:
+                    to = {"seq": lax.rem(z + dz, 4) * 16 + xy, "dp": lax.rem(core + dc, 2)}
+                    remote(sum1, mine, sent.at[11], came.at[11], to).start()
+
+    def gather():
+        first7 = phase2.at[pl.ds(0, 7)]
+        remote(first7, first7, sent.at[11], came.at[11], {"seq": me}).wait()
+        sum2[...] = jnp.sum(phase2[...], axis=0)
+        phase3[xy] = sum2[...]
+
+        def send(i, carry):
+            remote(sum2, phase3.at[xy], sent.at[12], came.at[12], {"seq": around(i)}).start()
+            return carry
+
+        lax.fori_loop(1, 16, send, 0)
+
+    def tap_sums(features):
+        def body(b, carry):
+            cols = lanes(b)
+            for i in features:
+                sums = []
+                for j in range(RIM + 1):
+                    both = ahead[i, 0, :ROWS, cols] * ext[i, 0, 8 - j : 8 - j + ROWS, cols]
+                    both = both + ahead[i, 1, :ROWS, cols] * ext[i, 1, 8 - j : 8 - j + ROWS, cols]
+                    sums.append(jnp.sum(both, axis=0, keepdims=True))
+                sums.append(jnp.zeros((1, LANES), FLOAT))
+                tiles[i * 8 + b] = jnp.concatenate(sums, axis=0)
+            return carry
+
+        lax.fori_loop(0, blocks, body, 0)
+
+    def raws(i):
+        def body(b, carry):
+            cols = lanes(b)
+            for w in range(2):
+                total = taps_ref[i, 0:1, cols] * ahead[i, w, :ROWS, cols]
+                for j in range(1, RIM + 1):
+                    total = total + taps_ref[i, j : j + 1, cols] * ahead[i, w, j : j + ROWS, cols]
+                raw_ref[i, w, :, cols] = total
+            return carry
+
+        lax.fori_loop(0, blocks, body, 0)
+        save = pltpu.make_async_copy(raw_ref.at[i], raw_hbm.at[i], saves.at[1 + i])
+        save.start()
+        return save
+
     peers_done(home, 3).wait_recv()
 
     def mix(b, carry):
         cols = lanes(b)
-        conv = home[pl.ds(pl.multiple_of(b * LANES, LANES), LANES), :].T
+        conv = home[lanes(b), :].T
         for w in range(2):
             part = conv[w * ROWS : (w + 1) * ROWS]
             mixed_ref[w, :, cols] = feat[0, w, :, cols] * part
@@ -445,6 +617,26 @@
         return carry
 
     lax.fori_loop(0, blocks, mix, 0)
+    packed(edge_q, ahead, (0,), 0)
+    after_q = remote(edge_q, after_q_rows, sent.at[9], came.at[9], {"seq": previous})
+    after_q.start()
+    save_mixed = pltpu.make_async_copy(mixed_ref, mixed_hbm, saves.at[0])
+    save_mixed.start()
+    tap_sums((0,))
+
+    outs_part = outs.at[:, pl.ds(0, 15)]
+    remote(outs_part, outs_part, sent.at[8], came.at[8], {"seq": me}).wait()
+    windows = 4
+    tail = 1.0 / math.sqrt(windows * SEQ)
+    scale = 4.0 / math.sqrt(windows * SEQ * blocks * LANES * 4)
+    for b in range(blocks):
+        rows = []
+        for s in range(8 * b, 8 * b + 8):
+            tile = outs[s // 16, s % 16]
+            rows += [tile, pltpu.roll(tile, ROWS, 1)]
+        square = jnp.concatenate(rows, axis=0).T
+        out_ref[:, b * LANES : (b + 1) * LANES] = square[:ROWS] * tail
+
     peers_done(home, 4).wait_recv()
 
     def unmix(b, carry):
@@ -457,87 +649,28 @@
         return carry
 
     lax.fori_loop(0, blocks, unmix, 0)
-    after = remote(
-        ahead.at[:, :, pl.ds(0, 8), :],
-        ahead.at[:, :, pl.ds(ROWS, 8), :],
-        sent.at[9],
-        came.at[9],
-        {"seq": lax.rem(me + ROWS - 1, ROWS)},
-    )
-    after.start()
-
-    def tap_sums(b, carry):
-        cols = lanes(b)
-        for i in range(3):
-            sums = []
-            for j in range(RIM + 1):
-                both = ahead[i, 0, :ROWS, cols] * ext[i, 0, 8 - j : 8 - j + ROWS, cols]
-                both = both + ahead[i, 1, :ROWS, cols] * ext[i, 1, 8 - j : 8 - j + ROWS, cols]
-                sums.append(jnp.sum(both, axis=0, keepdims=True))
-            sums.append(jnp.zeros((1, LANES), FLOAT))
-            tiles[i * 8 + b] = jnp.concatenate(sums, axis=0)
-        return carry
-
-    lax.fori_loop(0, blocks, tap_sums, 0)
-
-    phase1[xy] = tiles[pl.ds(2 * xy, 2)]
-
-    def scatter(i, carry):
-        q = around(i)
-        remote(tiles.at[pl.ds(2 * q, 2)], phase1.at[xy], sent.at[10], came.at[10], {"seq": z * 16 + q}).start()
-        return carry
-
-    lax.fori_loop(1, 16, scatter, 0)
-    after.wait()
-
-    @pl.when(me == ROWS - 1)
-    def _():
-        ahead[:, :, ROWS:, :] = jnp.zeros((3, 2, 8, ahead.shape[3]), FLOAT)
-
-    def raws(b, carry):
-        cols = lanes(b)
-        for i in range(3):
-            for w in range(2):
-                total = taps_ref[i, 0:1, cols] * ahead[i, w, :ROWS, cols]
-                for j in range(1, RIM + 1):
-                    total = total + taps_ref[i, j : j + 1, cols] * ahead[i, w, j : j + ROWS, cols]
-                raw_ref[i, w, :, cols] = total
-        return carry
-
-    lax.fori_loop(0, blocks, raws, 0)
-    first15 = phase1.at[pl.ds(0, 15)]
-    remote(first15, first15, sent.at[10], came.at[10], {"seq": me}).wait()
-    sum1[...] = jnp.sum(phase1[...], axis=0)
-    phase2[z * 2 + core] = sum1[...]
-    for dz in range(4):
-        for dc in range(2):
-            if dz or dc:
-                to = lax.rem(z + dz, 4) * 16 + xy
-                remote(sum1, phase2.at[z * 2 + core], sent.at[11], came.at[11], {"seq": to, "dp": lax.rem(core + dc, 2)}).start()
-    first7 = phase2.at[pl.ds(0, 7)]
-    remote(first7, first7, sent.at[11], came.at[11], {"seq": me}).wait()
-    sum2[...] = jnp.sum(phase2[...], axis=0)
-    phase3[xy] = sum2[...]
-
-    def gather(i, carry):
-        remote(sum2, phase3.at[xy], sent.at[12], came.at[12], {"seq": z * 16 + around(i)}).start()
-        return carry
-
-    lax.fori_loop(1, 16, gather, 0)
-
-    outs_part = outs.at[:, pl.ds(0, 15)]
-    remote(outs_part, outs_part, sent.at[8], came.at[8], {"seq": me}).wait()
-    windows = 4
-    tail = 1.0 / math.sqrt(windows * SEQ)
-    scale = 2.0 / math.sqrt(windows * SEQ * blocks * LANES * 4)
-    for b in range(blocks):
-        rows = []
-        for s in range(8 * b, 8 * b + 8):
-            tile = outs[s // 16, s % 16]
-            rows += [tile, pltpu.roll(tile, ROWS, 1)]
-        square = jnp.concatenate(rows, axis=0).T
-        out_ref[:, b * LANES : (b + 1) * LANES] = square[:ROWS] * tail
-
+    packed(edge_kv, ahead, keys, 0)
+    after_kv = remote(edge_kv, after_kv_rows, sent.at[14], came.at[14], {"seq": previous})
+    after_kv.start()
+    tap_sums(keys)
+    scatter()
+    after_q.wait()
+    unpacked(after_q_rows, ahead, (0,), ROWS)
+    no_rows(ahead, (0,), ROWS, ROWS - 1)
+    save_q = raws(0)
+    exchange()
+    after_kv.wait()
+    unpacked(after_kv_rows, ahead, keys, ROWS)
+    no_rows(ahead, keys, ROWS, ROWS - 1)
+    save_k = raws(1)
+    save_v = raws(2)
+    gather()
+    for sem in (1, 2):
+        peers_done(sends, sem).wait_send()
+    for sem in (3, 4):
+        peers_done(backs, sem).wait_send()
+    for save in (save_mixed, save_q, save_k, save_v):
+        save.wait()
     last15 = phase3.at[pl.ds(0, 15)]
     remote(last15, last15, sent.at[12], came.at[12], {"seq": me}).wait()
     for i in range(3):
@@ -548,20 +681,20 @@
     netf_ref[...] = net_sum[:32, :ROWS]
     nets_ref[:16, :] = net_sum[32:, :ROWS]
     nets_ref[16:, :] = net_sum[:, ROWS:]
-    for sem in (1, 2):
-        peers_done(sends, sem).wait_send()
-    for sem in (3, 4):
-        peers_done(backs, sem).wait_send()
 
 
 def shards(projected, short_weight, decay_rates, w1, w2, out_weight, cotangent):
     first_stack, last_stack, turn, middle, embedded = tables()
     vmem = pl.BlockSpec(memory_space=pltpu.VMEM)
+    hbm = pl.BlockSpec(memory_space=pl.ANY)
     group = projected.shape[3]
     hidden = w2.shape[0]
 
     def buffer(*shape):
         return pltpu.VMEM(shape, FLOAT)
+
+    def held(value):
+        return buffer(*value.shape)
 
     def like(value):
         return jax.ShapeDtypeStruct(value.shape, FLOAT)
@@ -577,9 +710,24 @@
             like(w1),
             like(w2),
         ),
-        in_specs=[pl.BlockSpec(memory_space=pltpu.SMEM), pl.BlockSpec(memory_space=pl.ANY)] + [vmem] * 10,
-        out_specs=(vmem,) * 6,
+        in_specs=[pl.BlockSpec(memory_space=pltpu.SMEM)] + [hbm] * 11,
+        out_specs=(hbm, hbm) + (vmem,) * 4,
         scratch_shapes=[
+            held(short_weight),
+            held(cotangent),
+            buffer(w1.shape[0], SEQ),
+            held(w1),
+            held(w2),
+            held(out_weight),
+            held(first_stack),
+            held(last_stack),
+            held(turn),
+            held(middle),
+            pltpu.VMEM(first_stack.shape, HALF),
+            pltpu.VMEM(last_stack.shape, HALF),
+            pltpu.VMEM(middle.shape, HALF),
+            held(cotangent),
+            held(projected),
             buffer(3, 2, rows, group),
             buffer(3, 2, rows, group),
             buffer(3, 2, ROWS, group),
@@ -594,8 +742,8 @@
             buffer(AREA, LANES),
             buffer(AREA, 2 * LANES),
             buffer(AREA, 2 * LANES),
-            buffer(56, LANES),
-            buffer(56, LANES),
+            buffer(8, LANES),
+            buffer(8, LANES),
             buffer(4, 48, LANES),
             buffer(4, 16, 8, LANES),
             buffer(32, 8, LANES),
@@ -606,12 +754,20 @@
             buffer(16, 2, 8, LANES),
             buffer(OWN, hidden),
             buffer(96, hidden),
-            pltpu.SemaphoreType.DMA,
-            pltpu.SemaphoreType.DMA((13,)),
-            pltpu.SemaphoreType.DMA((13,)),
+            buffer(24, group),
+            buffer(24, group),
+            buffer(24, group),
+            buffer(24, group),
+            buffer(16, group),
+            buffer(16, group),
+            buffer(16, group),
+            pltpu.SemaphoreType.DMA((11,)),
+            pltpu.SemaphoreType.DMA((4,)),
+            pltpu.SemaphoreType.DMA((18,)),
+            pltpu.SemaphoreType.DMA((18,)),
         ],
         compiler_params=pltpu.CompilerParams(
-            collective_id=1, has_side_effects=True, vmem_limit_bytes=52 << 20
+            collective_id=1, has_side_effects=True, vmem_limit_bytes=60 << 20
         ),
         name="whole",
     )(

time: 190 us -> 165 us (0.87)
  Pallas kernels: 174 us -> 156 us
  local copies, waits for them, and re-layouts: 12.6 us -> 7.24 us
    pallas_call x1, Pallas kernels: 174 us -> 156 us  [shards(): pl.pallas_call(whole_kernel, out_shape=(like(cotangent), like(projected),...]
    unnamed x22 -> x14, local copies, waits for them, and re-layouts: 12.6 us -> 7.24 us
where the time goes in v3:
time: 165 us; the launch traced here: 164 us
  Pallas kernels  156 us (95%)
  local copies, waits for them, and re-layouts  7.24 us (4%)
    pallas_call x1, Pallas kernels, shards(): pl.pallas_call(whole_kernel, out_shape=(like(cotangent), like(projected),...  156 us
    unnamed x14, local copies, waits for them, and re-layouts  7.24 us

profile of v3, /device:TPU:1, one launch (start us, length us, event | category | flops | bytes accessed | tf_op | source)
XLA Modules:
  0.0 163.6 jit_solution(9032468296007278032)
XLA Ops:
  0.6 155.7 %whole.1 = (f32[2,64,1024]{2,1,0:T(8,128)}, f32[3,2,64,1024]{3,2,1,0:T(8,128)}, f32[3,7,1024]{2,1,0:T(8,128)}, f32[64,1024]{1,0:T(8,128)}, f32[32,64]{1,0:T(8,128)}, /*index=5*/f32[64,64]{1,0:T(8,128)}) custom-call(f32[1024]{0:T(1024)} %rates_ref.1, f32[3,2,64,1024]{3,2,1,0:T(8,128)} %proj_hbm.1, f32[3,7,1024]{2,1,0:T(8,128)} %taps_hbm.1, ...), custom_call_target="tpu_custom_call" | custom-call | tf_op jit(solution)/shard_map/whole/pallas_call | solution.py:703
  156.3 1.9 %copy.24 = f32[2,64,1024]{2,1,0:T(8,128)} copy(f32[2,64,1024]{2,1,0:T(8,128)} %get-tuple-element.12) | data formatting | bytes 1048576
  158.2 0.0 copy-start.1
  158.2 0.0 copy-start
  158.2 0.0 copy-start.3
  158.2 0.0 copy-start.2
  158.2 2.8 %copy.25 = f32[3,2,64,1024]{3,2,1,0:T(8,128)} copy(f32[3,2,64,1024]{3,2,1,0:T(8,128)} %get-tuple-element.13) | data formatting | bytes 3145728
  161.0 0.0 copy-done.1
  161.0 0.6 copy.26
  161.7 0.0 copy-done
  161.7 0.7 copy.27
  162.4 0.0 copy-done.3
  162.4 0.6 copy.28
  163.0 0.0 copy-done.2
  163.0 0.6 copy.29
Async XLA Ops:
  158.2 2.8 %copy-start.1 = (f32[3,7,1024]{2,1,0:T(8,128)S(1)}, f32[3,7,1024]{2,1,0:T(8,128)}, u32[]{:S(2)}) copy-start(f32[3,7,1024]{2,1,0:T(8,128)} %get-tuple-element.14) | copy-start | bytes 258052
  158.2 3.4 %copy-start = (f32[64,1024]{1,0:T(8,128)S(1)}, f32[64,1024]{1,0:T(8,128)}, u32[]{:S(2)}) copy-start(f32[64,1024]{1,0:T(8,128)} %get-tuple-element.15) | copy-start | bytes 786436
  158.2 4.1 %copy-start.3 = (f32[32,64]{1,0:T(8,128)S(1)}, f32[32,64]{1,0:T(8,128)}, u32[]{:S(2)}) copy-start(f32[32,64]{1,0:T(8,128)} %get-tuple-element.16) | copy-start | bytes 24580
  158.2 4.7 %copy-start.2 = (f32[64,64]{1,0:T(8,128)S(1)}, f32[64,64]{1,0:T(8,128)}, u32[]{:S(2)}) copy-start(f32[64,64]{1,0:T(8,128)} %get-tuple-element.17) | copy-start | bytes 49156

commit v4 on v3

--- a/solution.py
+++ b/solution.py
@@ -195,7 +195,7 @@
     cos2,
     filt,
     fspec,
-    pspec,
+    gspec,
     out_mine,
     out_dp,
     by_chan,
@@ -210,7 +210,6 @@
     acc_net,
     edge_kv,
     rim_kv,
-    relay,
     after_kv_rows,
     edge_q,
     rim_q,
@@ -262,6 +261,7 @@
         copy.start()
     copies[0].wait()
     copies[1].wait()
+
     def lanes(b):
         return pl.ds(pl.multiple_of(b * LANES, LANES), LANES)
 
@@ -325,53 +325,14 @@
     later_rows((0,))
     pl.semaphore_wait(barrier, ROWS - 1 + 7)
 
-    quarter = edge_kv.shape[1] // 4
-    ahead_plane = lax.rem(z + 1, 4) * 16
-
-    def piece(ref, c):
-        return ref.at[:, c * quarter : (c + 1) * quarter]
-
-    @pl.when(xy != 15)
-    def _():
-        remote(edge_kv, rim_kv, sent.at[0], came.at[0], {"seq": following}).start()
-
-    @pl.when(xy == 15)
-    def _():
-        for c, via in enumerate((3, 12, 0)):
-            to = {"seq": z * 16 + via}
-            remote(piece(edge_kv, c), piece(relay, c), sent.at[0], came.at[16], to).start()
-        remote(piece(edge_kv, 3), piece(rim_kv, 3), sent.at[0], came.at[0], {"seq": following}).start()
-
-    for c, via in enumerate((3, 12, 0)):
-
-        @pl.when(xy == via)
-        def _(c=c):
-            part = piece(relay, c)
-            remote(part, part, sent.at[16], came.at[16], {"seq": me}).wait_recv()
-            on = remote(part, piece(rim_kv, c), sent.at[16], came.at[0], {"seq": ahead_plane})
-            on.start()
-            on.wait_send()
-
-    remote(rim_kv, rim_kv, sent.at[0], came.at[0], {"seq": me}).wait()
     to_q = remote(edge_q, rim_q, sent.at[13], came.at[13], {"seq": following})
+    to_kv = remote(edge_kv, rim_kv, sent.at[0], came.at[0], {"seq": following})
     to_q.start()
-    unpacked(rim_kv, ext, keys, 8 - RIM)
-    no_rows(ext, keys, 0, 0)
-
-    def products(b, carry):
-        cols = lanes(b)
-        for i in (1, 2):
-            for w in range(2):
-                tapped(i, w, cols, 0, 8)
-        parts = [feat[1, w, :, cols] * feat[2, w, :, cols] for w in range(2)]
-        sends[lanes(b), :] = jnp.concatenate(parts, axis=0).T
-        return carry
-
-    lax.fori_loop(0, blocks, products, 0)
-    to_peers(sends, got, 0, 1)
     to_q.wait()
+    to_kv.start()
     unpacked(rim_q, ext, (0,), 8 - RIM)
     no_rows(ext, (0,), 0, 0)
+
     copies[2].wait()
 
     def gradients(b, carry):
@@ -384,6 +345,7 @@
         return carry
 
     lax.fori_loop(0, blocks, gradients, 0)
+    to_peers(sends, got, 1, 2)
     for copy in copies[3:]:
         copy.wait()
     first_ref[...] = first_wide[...].astype(HALF)
@@ -444,7 +406,21 @@
         return carry
 
     lax.fori_loop(0, OWN // GROUP, filters, 0)
-    to_peers(sends, got, 1, 2)
+    to_kv.wait()
+    unpacked(rim_kv, ext, keys, 8 - RIM)
+    no_rows(ext, keys, 0, 0)
+
+    def products(b, carry):
+        cols = lanes(b)
+        for i in (1, 2):
+            for w in range(2):
+                tapped(i, w, cols, 0, 8)
+        parts = [feat[1, w, :, cols] * feat[2, w, :, cols] for w in range(2)]
+        sends[lanes(b), :] = jnp.concatenate(parts, axis=0).T
+        return carry
+
+    lax.fori_loop(0, blocks, products, 0)
+    to_peers(sends, got, 0, 1)
 
     def put(value, base, step):
         for i in range(GROUP):
@@ -452,37 +428,37 @@
                 :, i * LANES : (i + 1) * LANES
             ]
 
+    peers_done(got, 2).wait_recv()
+
+    def correlate(step, carry):
+        signals = [strided(got, AREA, step * GROUP + i) for i in range(GROUP)]
+        spec = forward(signals, first_ref, turn_ref, middle_ref)
+        gspec[group_rows(step), :] = spec
+        rows = cut(times_conj(fspec[group_rows(step), :], spec))
+        put(inverse(rows, last_ref, turn_ref, middle_ref), AREA, step)
+        return carry
+
+    lax.fori_loop(0, OWN // GROUP, correlate, 0)
+    to_peers(backs, home, 1, 4)
     peers_done(got, 1).wait_recv()
 
     def convolve(step, carry):
         signals = [strided(got, 0, step * GROUP + i) for i in range(GROUP)]
         spec = forward(signals, first_ref, turn_ref, middle_ref)
-        pspec[group_rows(step), :] = spec
         rows = cut(times(spec, fspec[group_rows(step), :]))
         put(inverse(rows, last_ref, turn_ref, middle_ref), 0, step)
+        pair = times_conj(spec, gspec[group_rows(step), :])
+        re, im = pair[:, :LANES], pair[:, LANES:]
+        gspec[group_rows(step), :] = columns(
+            [re + pltpu.roll(re, ROWS, 1), im + pltpu.roll(im, ROWS, 1)]
+        )
         return carry
 
     lax.fori_loop(0, OWN // GROUP, convolve, 0)
     to_peers(backs, home, 0, 3)
-    peers_done(got, 2).wait_recv()
-
-    def correlate(step, carry):
-        signals = [strided(got, AREA, step * GROUP + i) for i in range(GROUP)]
-        spec = forward(signals, first_ref, turn_ref, middle_ref)
-        rows = cut(times_conj(fspec[group_rows(step), :], spec))
-        put(inverse(rows, last_ref, turn_ref, middle_ref), AREA, step)
-        pair = times_conj(pspec[group_rows(step), :], spec)
-        re, im = pair[:, :LANES], pair[:, LANES:]
-        pspec[group_rows(step), :] = columns(
-            [re + pltpu.roll(re, ROWS, 1), im + pltpu.roll(im, ROWS, 1)]
-        )
-        return carry
-
-    lax.fori_loop(0, OWN // GROUP, correlate, 0)
-    to_peers(backs, home, 1, 4)
 
     def filter_back(step, carry):
-        rows = cut(pspec[group_rows(step), :])
+        rows = cut(gspec[group_rows(step), :])
         value = inverse(rows, last_ref, turn_ref, middle_ref)
         for i in range(GROUP):
             ch = step * GROUP + i
@@ -605,25 +581,6 @@
         save.start()
         return save
 
-    peers_done(home, 3).wait_recv()
-
-    def mix(b, carry):
-        cols = lanes(b)
-        conv = home[lanes(b), :].T
-        for w in range(2):
-            part = conv[w * ROWS : (w + 1) * ROWS]
-            mixed_ref[w, :, cols] = feat[0, w, :, cols] * part
-            ahead[0, w, :ROWS, cols] = cot_ref[w, :, cols] * part
-        return carry
-
-    lax.fori_loop(0, blocks, mix, 0)
-    packed(edge_q, ahead, (0,), 0)
-    after_q = remote(edge_q, after_q_rows, sent.at[9], came.at[9], {"seq": previous})
-    after_q.start()
-    save_mixed = pltpu.make_async_copy(mixed_ref, mixed_hbm, saves.at[0])
-    save_mixed.start()
-    tap_sums((0,))
-
     outs_part = outs.at[:, pl.ds(0, 15)]
     remote(outs_part, outs_part, sent.at[8], came.at[8], {"seq": me}).wait()
     windows = 4
@@ -653,17 +610,35 @@
     after_kv = remote(edge_kv, after_kv_rows, sent.at[14], came.at[14], {"seq": previous})
     after_kv.start()
     tap_sums(keys)
+    peers_done(home, 3).wait_recv()
+
+    def mix(b, carry):
+        cols = lanes(b)
+        conv = home[lanes(b), :].T
+        for w in range(2):
+            part = conv[w * ROWS : (w + 1) * ROWS]
+            mixed_ref[w, :, cols] = feat[0, w, :, cols] * part
+            ahead[0, w, :ROWS, cols] = cot_ref[w, :, cols] * part
+        return carry
+
+    lax.fori_loop(0, blocks, mix, 0)
+    packed(edge_q, ahead, (0,), 0)
+    after_q = remote(edge_q, after_q_rows, sent.at[9], came.at[9], {"seq": previous})
+    after_q.start()
+    save_mixed = pltpu.make_async_copy(mixed_ref, mixed_hbm, saves.at[0])
+    save_mixed.start()
+    tap_sums((0,))
     scatter()
-    after_q.wait()
-    unpacked(after_q_rows, ahead, (0,), ROWS)
-    no_rows(ahead, (0,), ROWS, ROWS - 1)
-    save_q = raws(0)
-    exchange()
     after_kv.wait()
     unpacked(after_kv_rows, ahead, keys, ROWS)
     no_rows(ahead, keys, ROWS, ROWS - 1)
     save_k = raws(1)
     save_v = raws(2)
+    exchange()
+    after_q.wait()
+    unpacked(after_q_rows, ahead, (0,), ROWS)
+    no_rows(ahead, (0,), ROWS, ROWS - 1)
+    save_q = raws(0)
     gather()
     for sem in (1, 2):
         peers_done(sends, sem).wait_send()
@@ -683,6 +658,24 @@
     nets_ref[16:, :] = net_sum[:, ROWS:]
 
 
+def land_kernel(*refs):
+    count = (len(refs) - 1) // 2
+    sems = refs[-1]
+    pairs = []
+    for source, target in zip(refs[:count], refs[count : 2 * count]):
+        if len(source.shape) == 4:
+            pairs += [(source.at[i, w], target.at[i, w]) for i in range(3) for w in range(2)]
+        elif source.shape[0] == 2:
+            pairs += [(source.at[w], target.at[w]) for w in range(2)]
+        else:
+            pairs.append((source, target))
+    copies = [pltpu.make_async_copy(*pair, sems.at[n]) for n, pair in enumerate(pairs)]
+    for copy in copies:
+        copy.start()
+    for copy in copies:
+        copy.wait()
+
+
 def shards(projected, short_weight, decay_rates, w1, w2, out_weight, cotangent):
     first_stack, last_stack, turn, middle, embedded = tables()
     vmem = pl.BlockSpec(memory_space=pltpu.VMEM)
@@ -700,7 +693,7 @@
         return jax.ShapeDtypeStruct(value.shape, FLOAT)
 
     rows = projected.shape[2] + 8
-    return pl.pallas_call(
+    results = pl.pallas_call(
         whole_kernel,
         out_shape=(
             like(cotangent),
@@ -757,7 +750,6 @@
             buffer(24, group),
             buffer(24, group),
             buffer(24, group),
-            buffer(24, group),
             buffer(16, group),
             buffer(16, group),
             buffer(16, group),
@@ -784,6 +776,15 @@
         jnp.asarray(turn),
         jnp.asarray(middle),
     )
+    return pl.pallas_call(
+        land_kernel,
+        out_shape=tuple(like(v) for v in results),
+        in_specs=[hbm] * len(results),
+        out_specs=(hbm,) * len(results),
+        scratch_shapes=[pltpu.SemaphoreType.DMA((12,))],
+        compiler_params=pltpu.CompilerParams(vmem_limit_bytes=60 << 20),
+        name="land",
+    )(*results)
 
 
 def solution(mesh):

time: 165 us -> 242 us (1.47)
  Pallas kernels: 156 us -> 241 us
  local copies, waits for them, and re-layouts: 7.24 us -> 0 us
    pallas_call x0 -> x1, Pallas kernels: none -> 77.1 us  [shards(): pl.pallas_call(land_kernel, out_shape=tuple((like(v) for v in results)),...]
    pallas_call x1, Pallas kernels: 156 us -> 164 us  [shards(): pl.pallas_call(whole_kernel, out_shape=(like(cotangent), like(projected),...]
    unnamed x14 -> x0, local copies, waits for them, and re-layouts: 7.24 us -> none
where the time goes in v4:
time: 242 us
  Pallas kernels  241 us (100%)
    pallas_call x1, Pallas kernels, shards(): pl.pallas_call(whole_kernel, out_shape=(like(cotangent), like(projected),...  164 us
    pallas_call x1, Pallas kernels, shards(): pl.pallas_call(land_kernel, out_shape=tuple((like(v) for v in results)),...  77.1 us

profile of v4, /device:TPU:1, one launch (start us, length us, event | category | flops | bytes accessed | tf_op | source)
XLA Modules:
  0.0 242.0 jit_solution(10571330274213274929)
XLA Ops:
  0.6 164.2 %whole.1 = (f32[2,64,1024]{2,1,0:T(8,128)}, f32[3,2,64,1024]{3,2,1,0:T(8,128)}, f32[3,7,1024]{2,1,0:T(8,128)}, f32[64,1024]{1,0:T(8,128)}, f32[32,64]{1,0:T(8,128)}, /*index=5*/f32[64,64]{1,0:T(8,128)}) custom-call(f32[1024]{0:T(1024)} %rates_ref.1, f32[3,2,64,1024]{3,2,1,0:T(8,128)} %proj_hbm.1, f32[3,7,1024]{2,1,0:T(8,128)} %taps_hbm.1, ...), custom_call_target="tpu_custom_call" | custom-call | tf_op jit(solution)/shard_map/whole/pallas_call | solution.py:696
  164.8 77.1 %land.1 = (f32[2,64,1024]{2,1,0:T(8,128)}, f32[3,2,64,1024]{3,2,1,0:T(8,128)}, f32[3,7,1024]{2,1,0:T(8,128)}, f32[64,1024]{1,0:T(8,128)}, f32[32,64]{1,0:T(8,128)}, /*index=5*/f32[64,64]{1,0:T(8,128)}) custom-call(f32[2,64,1024]{2,1,0:T(8,128)} %get-tuple-element.12.refs_0_, f32[3,2,64,1024]{3,2,1,0:T(8,128)} %get-tuple-element.13.refs_1_, ...), custom_call_target="tpu_custom_call" | custom-call | tf_op jit(solution)/shard_map/land/pallas_call | solution.py:779

commit v5 on v3

--- a/solution.py
+++ b/solution.py
@@ -196,6 +196,7 @@
     filt,
     fspec,
     pspec,
+    gspec,
     out_mine,
     out_dp,
     by_chan,
@@ -262,6 +263,7 @@
         copy.start()
     copies[0].wait()
     copies[1].wait()
+
     def lanes(b):
         return pl.ds(pl.multiple_of(b * LANES, LANES), LANES)
 
@@ -471,18 +473,16 @@
         spec = forward(signals, first_ref, turn_ref, middle_ref)
         rows = cut(times_conj(fspec[group_rows(step), :], spec))
         put(inverse(rows, last_ref, turn_ref, middle_ref), AREA, step)
-        pair = times_conj(pspec[group_rows(step), :], spec)
-        re, im = pair[:, :LANES], pair[:, LANES:]
-        pspec[group_rows(step), :] = columns(
-            [re + pltpu.roll(re, ROWS, 1), im + pltpu.roll(im, ROWS, 1)]
-        )
+        gspec[group_rows(step), :] = spec
         return carry
 
     lax.fori_loop(0, OWN // GROUP, correlate, 0)
     to_peers(backs, home, 1, 4)
 
     def filter_back(step, carry):
-        rows = cut(pspec[group_rows(step), :])
+        pair = times_conj(pspec[group_rows(step), :], gspec[group_rows(step), :])
+        re, im = pair[:, :LANES], pair[:, LANES:]
+        rows = cut(columns([re + pltpu.roll(re, ROWS, 1), im + pltpu.roll(im, ROWS, 1)]))
         value = inverse(rows, last_ref, turn_ref, middle_ref)
         for i in range(GROUP):
             ch = step * GROUP + i
@@ -683,6 +683,35 @@
     nets_ref[16:, :] = net_sum[:, ROWS:]
 
 
+def land_kernel(*refs):
+    count = (len(refs) - 2) // 3
+    sources, targets, held = refs[:count], refs[count : 2 * count], refs[2 * count : 3 * count]
+    loads, stores = refs[3 * count :]
+    pieces = []
+    for n, source in enumerate(sources):
+        lead = source.shape[:-2]
+        pieces += [(n, at) for at in np.ndindex(*lead)] if source.shape[-2] == ROWS else [(n, ())]
+
+    def part(ref, at):
+        return ref.at[at] if at else ref
+
+    first = [
+        pltpu.make_async_copy(part(sources[n], at), part(held[n], at), loads.at[k])
+        for k, (n, at) in enumerate(pieces)
+    ]
+    second = [
+        pltpu.make_async_copy(part(held[n], at), part(targets[n], at), stores.at[k])
+        for k, (n, at) in enumerate(pieces)
+    ]
+    for copy in first:
+        copy.start()
+    for load, store in zip(first, second):
+        load.wait()
+        store.start()
+    for copy in second:
+        copy.wait()
+
+
 def shards(projected, short_weight, decay_rates, w1, w2, out_weight, cotangent):
     first_stack, last_stack, turn, middle, embedded = tables()
     vmem = pl.BlockSpec(memory_space=pltpu.VMEM)
@@ -700,7 +729,7 @@
         return jax.ShapeDtypeStruct(value.shape, FLOAT)
 
     rows = projected.shape[2] + 8
-    return pl.pallas_call(
+    results = pl.pallas_call(
         whole_kernel,
         out_shape=(
             like(cotangent),
@@ -740,6 +769,7 @@
             buffer(hidden, SEQ),
             buffer(hidden, SEQ),
             buffer(AREA, LANES),
+            buffer(AREA, 2 * LANES),
             buffer(AREA, 2 * LANES),
             buffer(AREA, 2 * LANES),
             buffer(8, LANES),
@@ -784,6 +814,16 @@
         jnp.asarray(turn),
         jnp.asarray(middle),
     )
+    return pl.pallas_call(
+        land_kernel,
+        out_shape=tuple(like(v) for v in results),
+        in_specs=[hbm] * len(results),
+        out_specs=(hbm,) * len(results),
+        scratch_shapes=[held(v) for v in results]
+        + [pltpu.SemaphoreType.DMA((16,)), pltpu.SemaphoreType.DMA((16,))],
+        compiler_params=pltpu.CompilerParams(vmem_limit_bytes=60 << 20),
+        name="land",
+    )(*results)
 
 
 def solution(mesh):

time: 165 us -> 160 us (0.970)
  local copies, waits for them, and re-layouts: 7.24 us -> 0 us
  Pallas kernels: 156 us -> 158 us
    unnamed x14 -> x0, local copies, waits for them, and re-layouts: 7.24 us -> none
    pallas_call x0 -> x1, Pallas kernels: none -> 2.66 us  [shards(): pl.pallas_call(land_kernel, out_shape=tuple((like(v) for v in results)),...]
where the time goes in v5:
time: 160 us; the launch traced here: 159 us
  Pallas kernels  158 us (99%)
    pallas_call x1, Pallas kernels, shards(): pl.pallas_call(whole_kernel, out_shape=(like(cotangent), like(projected),...  156 us

profile of v5, /device:TPU:1, one launch (start us, length us, event | category | flops | bytes accessed | tf_op | source)
XLA Modules:
  0.0 159.0 jit_solution(800945196332193311)
XLA Ops:
  0.6 155.7 %whole.1 = (f32[2,64,1024]{2,1,0:T(8,128)}, f32[3,2,64,1024]{3,2,1,0:T(8,128)}, f32[3,7,1024]{2,1,0:T(8,128)}, f32[64,1024]{1,0:T(8,128)}, f32[32,64]{1,0:T(8,128)}, /*index=5*/f32[64,64]{1,0:T(8,128)}) custom-call(f32[1024]{0:T(1024)} %rates_ref.1, f32[3,2,64,1024]{3,2,1,0:T(8,128)} %proj_hbm.1, f32[3,7,1024]{2,1,0:T(8,128)} %taps_hbm.1, ...), custom_call_target="tpu_custom_call" | custom-call | tf_op jit(solution)/shard_map/whole/pallas_call | solution.py:732
  156.3 2.7 %land.1 = (f32[2,64,1024]{2,1,0:T(8,128)}, f32[3,2,64,1024]{3,2,1,0:T(8,128)}, f32[3,7,1024]{2,1,0:T(8,128)}, f32[64,1024]{1,0:T(8,128)}, f32[32,64]{1,0:T(8,128)}, /*index=5*/f32[64,64]{1,0:T(8,128)}) custom-call(f32[2,64,1024]{2,1,0:T(8,128)} %get-tuple-element.12.refs_0_, f32[3,2,64,1024]{3,2,1,0:T(8,128)} %get-tuple-element.13.refs_1_, ...), custom_call_target="tpu_custom_call" | custom-call | tf_op jit(solution)/shard_map/land/pallas_call | solution.py:817

commit v6 on v5

--- a/solution.py
+++ b/solution.py
@@ -289,6 +289,7 @@
         target[mine, :] = source[mine, :]
 
         def send(i, carry):
+            i = lax.rem(i - 1 + 31 * core + 5 * xy, ROWS - 1) + 1
             px, py = lax.rem(x + lax.rem(i // 4, 4), 4), lax.rem(y + i // 16, 4)
             peer = lax.rem(z + lax.rem(i, 4), 4) * 16 + px * 4 + py
             block = pl.ds(pl.multiple_of(base + peer * OWN, OWN), OWN)

time: 160 us -> 158 us (0.988); the launches traced: 159 us -> 155 us
  Pallas kernels: 158 us -> 155 us
    pallas_call x1, Pallas kernels: 156 us -> 152 us  [shards(): pl.pallas_call(whole_kernel, out_shape=(like(cotangent), like(projected),...]
where the time goes in v6:
time: 158 us; the launch traced here: 155 us
  Pallas kernels  155 us (98%)
    pallas_call x1, Pallas kernels, shards(): pl.pallas_call(whole_kernel, out_shape=(like(cotangent), like(projected),...  152 us

profile of v6, /device:TPU:1, one launch (start us, length us, event | category | flops | bytes accessed | tf_op | source)
XLA Modules:
  0.0 155.2 jit_solution(13521764331484783435)
XLA Ops:
  0.6 151.9 %whole.1 = (f32[2,64,1024]{2,1,0:T(8,128)}, f32[3,2,64,1024]{3,2,1,0:T(8,128)}, f32[3,7,1024]{2,1,0:T(8,128)}, f32[64,1024]{1,0:T(8,128)}, f32[32,64]{1,0:T(8,128)}, /*index=5*/f32[64,64]{1,0:T(8,128)}) custom-call(f32[1024]{0:T(1024)} %rates_ref.1, f32[3,2,64,1024]{3,2,1,0:T(8,128)} %proj_hbm.1, f32[3,7,1024]{2,1,0:T(8,128)} %taps_hbm.1, ...), custom_call_target="tpu_custom_call" | custom-call | tf_op jit(solution)/shard_map/whole/pallas_call | solution.py:733
  152.5 2.7 %land.1 = (f32[2,64,1024]{2,1,0:T(8,128)}, f32[3,2,64,1024]{3,2,1,0:T(8,128)}, f32[3,7,1024]{2,1,0:T(8,128)}, f32[64,1024]{1,0:T(8,128)}, f32[32,64]{1,0:T(8,128)}, /*index=5*/f32[64,64]{1,0:T(8,128)}) custom-call(f32[2,64,1024]{2,1,0:T(8,128)} %get-tuple-element.12.refs_0_, f32[3,2,64,1024]{3,2,1,0:T(8,128)} %get-tuple-element.13.refs_1_, ...), custom_call_target="tpu_custom_call" | custom-call | tf_op jit(solution)/shard_map/land/pallas_call | solution.py:818

commit v7 on v5

--- a/solution.py
+++ b/solution.py
@@ -289,6 +289,7 @@
         target[mine, :] = source[mine, :]
 
         def send(i, carry):
+            i = lax.rem(i - 1 + 31 * core + 5 * xy + 17 * chan, ROWS - 1) + 1
             px, py = lax.rem(x + lax.rem(i // 4, 4), 4), lax.rem(y + i // 16, 4)
             peer = lax.rem(z + lax.rem(i, 4), 4) * 16 + px * 4 + py
             block = pl.ds(pl.multiple_of(base + peer * OWN, OWN), OWN)

time: 160 us -> 160 us (level)
  no operation moved by 1% of the time
where the time goes in v7:
time: 160 us; the launch traced here: 158 us
  Pallas kernels  157 us (98%)
    pallas_call x1, Pallas kernels, shards(): pl.pallas_call(whole_kernel, out_shape=(like(cotangent), like(projected),...  155 us

profile of v7, /device:TPU:1, one launch (start us, length us, event | category | flops | bytes accessed | tf_op | source)
XLA Modules:
  0.0 157.9 jit_solution(434252158261817826)
XLA Ops:
  0.6 154.6 %whole.1 = (f32[2,64,1024]{2,1,0:T(8,128)}, f32[3,2,64,1024]{3,2,1,0:T(8,128)}, f32[3,7,1024]{2,1,0:T(8,128)}, f32[64,1024]{1,0:T(8,128)}, f32[32,64]{1,0:T(8,128)}, /*index=5*/f32[64,64]{1,0:T(8,128)}) custom-call(f32[1024]{0:T(1024)} %rates_ref.1, f32[3,2,64,1024]{3,2,1,0:T(8,128)} %proj_hbm.1, f32[3,7,1024]{2,1,0:T(8,128)} %taps_hbm.1, ...), custom_call_target="tpu_custom_call" | custom-call | tf_op jit(solution)/shard_map/whole/pallas_call | solution.py:733
  155.2 2.7 %land.1 = (f32[2,64,1024]{2,1,0:T(8,128)}, f32[3,2,64,1024]{3,2,1,0:T(8,128)}, f32[3,7,1024]{2,1,0:T(8,128)}, f32[64,1024]{1,0:T(8,128)}, f32[32,64]{1,0:T(8,128)}, /*index=5*/f32[64,64]{1,0:T(8,128)}) custom-call(f32[2,64,1024]{2,1,0:T(8,128)} %get-tuple-element.12.refs_0_, f32[3,2,64,1024]{3,2,1,0:T(8,128)} %get-tuple-element.13.refs_1_, ...), custom_call_target="tpu_custom_call" | custom-call | tf_op jit(solution)/shard_map/land/pallas_call | solution.py:818
